TPU v7x, 128 devices: a whole 4x4x4 slice. The times are simulated.
128 devices in a mesh: section: 4 (over z), seq: 16 (over y, x), mp: 2 (over core).
Axes of the slice: x: 4, y: 4, z: 4, core: 2. Of those that a mesh axis runs over, the one named last changes fastest.
Arguments:
- fresh_input: bfloat16 [4, 8192, 2048], P('section', 'seq', 'mp'), may hold values from -6 to 6
- saved_input: bfloat16 [4, 8192, 2048], P('section', 'seq', 'mp'), may hold values from -6 to 6
- cotangent: bfloat16 [4, 8192, 2048], P('section', 'seq', 'mp'), may hold values from -4 to 4
- factor_one: bfloat16 [4, 32, 256, 256], P('section', 'seq'), may hold values from -0.375 to 0.375
- twiddle: bfloat16 [4, 256, 2048], P('section', None, 'mp'), may hold values from -4 to 4
- factor_two: bfloat16 [4, 256, 32, 32], P('section', 'seq'), may hold values from -1 to 1
- up_weight: bfloat16 [4, 4, 512, 2048], P('section', 'mp'), may hold values from -0.25 to 0.25
- down_weight: bfloat16 [4, 4, 2048, 512], P('section', 'mp'), may hold values from -0.125 to 0.125
Outputs:
- sent_activation: bfloat16 [4, 8192, 2048], P('section', 'seq', 'mp')
- sent_gradient: bfloat16 [4, 8192, 2048], P('section', 'seq', 'mp')
- up_gradient: float32 [4, 4, 512, 2048], P('section', 'mp', 'seq')
- down_gradient: float32 [4, 4, 2048, 512], P('section', 'mp', 'seq')
- twiddle_gradient: float32 [4, 256, 2048], P('section', 'seq', 'mp')
- first_gradient: float32 [4, 32, 256, 256], P('section', 'seq')
- second_gradient: float32 [4, 256, 32, 32], P('section', 'seq')
All inputs are finite; a program needn't handle non-finite values.
Results may differ from a plain program's by a relative error of at most 0.01.
Values may be sent and summed in bfloat16 or wider, within the bound.
A program may use at most 128 MiB of HBM per device.

v0:
```python
import jax
import jax.numpy as jnp
from jax import lax
from jax.sharding import PartitionSpec as P


def passed_along(x, axis, by):
    size = lax.axis_size(axis)
    pairs = [(i, i + by) for i in range(size) if 0 <= i + by < size]
    return lax.ppermute(x, axis, pairs)


def gelu_tanh(values):
    return jax.nn.gelu(values, approximate=True)


def first_factor(inputs, factor_first, twist):
    inner_sum = jnp.einsum(
        "abk,makc->mabc", factor_first, inputs, preferred_element_type=jnp.float32
    )
    twisted = (inner_sum * twist.astype(jnp.float32)).astype(jnp.bfloat16)
    return (inner_sum, twisted)


def second_factor(columns, factor_second):
    return jnp.einsum(
        "bij,mjbc->mibc", factor_second, columns, preferred_element_type=jnp.float32
    ).astype(jnp.bfloat16)


def channel_forward(inputs, mixed, up_local, down_local):
    tokens, width_local = inputs.shape
    groups, block_width, hidden_width = up_local.shape
    gating = jax.nn.sigmoid(inputs.astype(jnp.float32))
    hidden = (inputs.astype(jnp.float32) + mixed.astype(jnp.float32) * gating).astype(jnp.bfloat16)
    lifted = jnp.einsum(
        "tkd,kdf->tkf",
        hidden.reshape(tokens, groups, block_width),
        up_local,
        preferred_element_type=jnp.float32,
    )
    activated = gelu_tanh(lifted).astype(jnp.bfloat16)
    projected = jnp.einsum(
        "tkf,kfd->tkd", activated, down_local, preferred_element_type=jnp.float32
    )
    result = (hidden.astype(jnp.float32) + projected.reshape(tokens, width_local)).astype(
        jnp.bfloat16
    )
    return (gating, hidden, lifted, activated, result)


def body(
    fresh_input, saved_input, cotangent, factor_one, twiddle, factor_two, up_weight, down_weight
):
    fresh_rows = fresh_input[0]
    saved_rows = saved_input[0]
    incoming = cotangent[0]
    first = factor_one[0]
    twist = twiddle[0]
    second = factor_two[0]
    up_local = up_weight[0]
    down_local = down_weight[0]
    tokens, width_local = fresh_rows.shape
    blocks_here = first.shape[0]
    block_size = first.shape[1]
    groups, block_width, hidden_width = up_local.shape

    def mix_single(columns):
        return (
            lax.all_to_all(
                second_factor(columns, second), "seq", split_axis=1, concat_axis=2, tiled=True
            ),
            columns,
        )

    def run_mixer(rows):
        inner_sum, twisted = first_factor(
            rows.reshape(1, blocks_here, block_size, width_local), first, twist
        )
        mixed, columns = mix_single(
            lax.all_to_all(twisted, "seq", split_axis=2, concat_axis=1, tiled=True)
        )
        return (inner_sum[0], mixed[0], columns[0])

    fresh_mixed = run_mixer(fresh_rows)[1]
    saved_parts = run_mixer(saved_rows)
    saved_inner = saved_parts[0]
    saved_mixed = saved_parts[1]
    saved_columns = saved_parts[2]
    fresh_result = channel_forward(
        fresh_rows, fresh_mixed.reshape(tokens, width_local), up_local, down_local
    )[4]
    sent_rows = passed_along(fresh_result, "section", 1)
    saved_flat = saved_mixed.reshape(tokens, width_local)
    saved_state = channel_forward(saved_rows, saved_flat, up_local, down_local)
    gating = saved_state[0]
    hidden = saved_state[1]
    lifted = saved_state[2]
    activated = saved_state[3]
    incoming_blocks = incoming.reshape(tokens, groups, block_width)
    back_act = jnp.einsum(
        "tkd,kfd->tkf", incoming_blocks, down_local, preferred_element_type=jnp.float32
    )
    d_lifted = jax.vjp(gelu_tanh, lifted)[1](back_act)[0].astype(jnp.bfloat16)
    down_grad = jnp.einsum(
        "tkf,tkd->kfd", activated, incoming_blocks, preferred_element_type=jnp.float32
    )
    up_grad = jnp.einsum(
        "tkd,tkf->kdf",
        hidden.reshape(tokens, groups, block_width),
        d_lifted,
        preferred_element_type=jnp.float32,
    )
    d_hidden = incoming.astype(jnp.float32) + jnp.einsum(
        "tkf,kdf->tkd", d_lifted, up_local, preferred_element_type=jnp.float32
    ).reshape(tokens, width_local)
    d_mixed = (d_hidden * gating).astype(jnp.bfloat16).reshape(blocks_here, block_size, width_local)
    grad_cols = lax.all_to_all(d_mixed, "seq", split_axis=1, concat_axis=0, tiled=True)
    second_grad = jnp.einsum(
        "ibc,jbc->bij", grad_cols, saved_columns, preferred_element_type=jnp.float32
    )
    d_twisted = jnp.einsum(
        "bij,ibc->jbc", second, grad_cols, preferred_element_type=jnp.float32
    ).astype(jnp.bfloat16)
    d_rows = lax.all_to_all(d_twisted, "seq", split_axis=0, concat_axis=1, tiled=True)
    twiddle_grad = jnp.sum(d_rows.astype(jnp.float32) * saved_inner, axis=0)
    d_inner = (d_rows.astype(jnp.float32) * twist.astype(jnp.float32)).astype(jnp.bfloat16)
    saved_blocks = saved_rows.reshape(blocks_here, block_size, width_local)
    first_grad = jnp.einsum(
        "abc,akc->abk", d_inner, saved_blocks, preferred_element_type=jnp.float32
    )
    local_back = jnp.einsum(
        "abk,abc->akc", first, d_inner, preferred_element_type=jnp.float32
    ).reshape(tokens, width_local)
    direct = d_hidden * (1.0 + saved_flat.astype(jnp.float32) * gating * (1.0 - gating))
    d_input = (direct + local_back).astype(jnp.bfloat16)
    sent_back = passed_along(d_input, "section", -1)
    first_sum, second_sum = lax.psum((first_grad, second_grad), "mp")
    up_share, down_share, twiddle_share = (
        lax.psum_scatter(up_grad, "seq", scatter_dimension=1, tiled=True),
        lax.psum_scatter(down_grad, "seq", scatter_dimension=1, tiled=True),
        lax.psum_scatter(twiddle_grad[None], "seq", scatter_dimension=1, tiled=True),
    )
    return (
        sent_rows[None],
        sent_back[None],
        up_share[None],
        down_share[None],
        twiddle_share[0][None],
        first_sum[None],
        second_sum[None],
    )


def solution(mesh):
    return jax.shard_map(
        body,
        mesh=mesh,
        in_specs=(
            P("section", "seq", "mp"),
            P("section", "seq", "mp"),
            P("section", "seq", "mp"),
            P("section", "seq", None, None),
            P("section", None, "mp"),
            P("section", "seq", None, None),
            P("section", "mp", None, None),
            P("section", "mp", None, None),
        ),
        out_specs=(
            P("section", "seq", "mp"),
            P("section", "seq", "mp"),
            P("section", "mp", "seq", None),
            P("section", "mp", "seq", None),
            P("section", "seq", "mp"),
            P("section", "seq", None, None),
            P("section", "seq", None, None),
        ),
        check_vma=False,
    )
```

profile of v0, /device:TPU:1, one launch (start us, length us, event | category | flops | bytes accessed | tf_op | source)
XLA Modules:
  0.0 455.3 jit_solution(15085247805249956167)
XLA Ops:
  8.8 2.2 fusion.37
  11.1 2.6 copy.299
  13.7 23.5 %all_to_all.75 = bf16[1,2,256,1024]{3,1,0,2:T(2,128)(2,1)S(1)} all-to-all(bf16[1,2,256,1024]{3,1,0,2:T(2,128)(2,1)S(1)} %copy.299), channel_id=1, replica_groups=mesh['section'=4,'seq'=16,'mp'=2] {'seq'}, dimensions={2} | all-to-all | bytes 2097152 | tf_op jit(solution)/shard_map/all_to_all | solution.py:81
  39.4 1.6 copy.302
  41.0 3.7 all-to-all-start.3
  45.2 1.7 copy.297
  46.9 3.1 copy.307
  49.9 1.6 reshape_squeeze.2
  51.5 8.2 %all-to-all-done.3 = bf16[1,32,16,1024]{3,2,0,1:T(8,128)(2,1)S(1)} async-done(((bf16[1,32,16,1024]{3,2,0,1:T(8,128)(2,1)}), bf16[1,32,16,1024]{3,2,0,1:T(8,128)(2,1)S(1)}, u32[]{:S(2)}, u32[]{:S(2)}) %all-to-all-start.3) | async-done | bytes 1048608 | tf_op jit(solution)/shard_map/all_to_all | solution.py:70
  60.2 2.8 reshape.120
  63.0 3.3 fusion.47
  67.4 2.4 fusion.27
  69.9 7.2 %fusion.6 = bf16[512,2,2048]{2,0,1:T(8,128)(2,1)S(1)} fusion(f32[2,512,2048]{2,1,0:T(8,128)S(1)} %fusion.27, bf16[1,2,2048,512]{3,2,1,0:T(8,128)(2,1)S(1)} %copy-done.29, bf16[512,2,512]{2,1,0:T(2,128)(2,1)S(1)} %copy-done.25), kind=kOutput, calls=%fused_computation.9 | convolution fusion | flops 2189426688 | bytes 17825792 | tf_op jit(solution)/shard_map/tkd,kfd->tkf/dot_general | solution.py:101
  77.1 2.4 fusion.25
  79.5 1.4 copy-done.19
  80.8 2.4 reshape.111
  83.2 4.2 copy.310
  87.5 2.2 multiply_convert_fusion.1
  90.8 20.6 %all_to_all.76 = bf16[2,256,1024]{2,0,1:T(2,128)(2,1)S(1)} all-to-all(bf16[2,256,1024]{2,0,1:T(2,128)(2,1)S(1)} %copy.311), channel_id=1, replica_groups=mesh['section'=4,'seq'=16,'mp'=2] {'seq'}, dimensions={1} | all-to-all | bytes 2097152 | tf_op jit(solution)/shard_map/all_to_all | solution.py:118
  113.9 18.3 %all_to_all.77 = bf16[32,16,1024]{2,1,0:T(8,128)(2,1)S(1)} all-to-all(bf16[32,16,1024]{2,1,0:T(8,128)(2,1)S(1)} %copy.314), channel_id=1, replica_groups=mesh['section'=4,'seq'=16,'mp'=2] {'seq'}, dimensions={0} | all-to-all | bytes 2097152 | tf_op jit(solution)/shard_map/all_to_all | solution.py:125
  132.7 1.9 copy.320
  134.7 3.6 fusion.34
  138.3 3.6 copy.321
  142.0 2.7 convolution_bitcast_fusion.1
  147.4 7.8 %fusion.80 = f32[2,512,2048]{2,1,0:T(8,128)} fusion(bf16[512,2,512]{2,0,1:T(8,128)(2,1)S(1)} %copy-done.6, bf16[512,2,2048]{2,0,1:T(8,128)(2,1)} %copy-done.23), kind=kOutput, calls=%fused_computation.102 | convolution fusion | flops 2147483648 | bytes 13631488 | tf_op jit(solution)/shard_map/tkd,tkf->kdf/dot_general | solution.py:108
  156.5 10.1 %fusion.19 = f32[2,2048,512]{2,1,0:T(8,128)} fusion(f32[2,512,2048]{2,1,0:T(8,128)} %copy-done.2, bf16[512,2,512]{2,1,0:T(2,128)(2,1)S(1)} %copy-done.26), kind=kOutput, calls=%fused_computation.25 | convolution fusion | flops 2166358016 | bytes 17825792 | tf_op jit(solution)/shard_map/tkf,tkd->kfd/dot_general | solution.py:105
  168.1 1.5 fusion.36
  169.6 2.6 copy.282
  172.2 17.2 %all_to_all.78 = bf16[1,2,256,1024]{3,1,0,2:T(2,128)(2,1)S(1)} all-to-all(bf16[1,2,256,1024]{3,1,0,2:T(2,128)(2,1)S(1)} %copy.282), channel_id=1, replica_groups=mesh['section'=4,'seq'=16,'mp'=2] {'seq'}, dimensions={2} | all-to-all | bytes 2097152 | tf_op jit(solution)/shard_map/all_to_all | solution.py:81
  192.0 1.6 fusion.53
  193.6 1.5 copy.285
  195.2 4.3 all-to-all-start.1
  199.5 1.7 copy.288
  201.2 3.0 copy.292
  204.2 1.8 copy.308
  206.1 7.6 %all-to-all-done.1 = bf16[1,32,16,1024]{3,2,0,1:T(8,128)(2,1)} async-done(((bf16[1,32,16,1024]{3,2,0,1:T(8,128)(2,1)}), bf16[1,32,16,1024]{3,2,0,1:T(8,128)(2,1)}, u32[]{:S(2)}, u32[]{:S(2)}) %all-to-all-start.1) | async-done | bytes 1048608 | tf_op jit(solution)/shard_map/all_to_all | solution.py:70
  213.6 1.5 convert_bitcast_fusion.2
  215.4 2.9 reshape.117
  218.3 11.3 %fusion.23 = f32[2,512,512]{1,2,0:T(8,128)} fusion(bf16[1,2,2048,512]{3,2,1,0:T(8,128)(2,1)} %param.15, bf16[1,2,512,2048]{3,2,1,0:T(8,128)(2,1)} %param.14, f32[512,2,512]{2,0,1:T(8,128)} %copy.292, f32[512,2,512]{2,1,0:T(2,128)} %reshape.117), kind=kOutput, calls=%fused_computation.28 | convolution fusion | flops 4316987392 | bytes 14680064 | tf_op jit(solution)/shard_map/tkf,kfd->tkd/dot_general | solution.py:43
  229.6 2.9 copy.294
  232.5 3.8 add_convert_fusion
  236.3 3.7 collective-permute-start
  241.6 1.3 collective-permute-start.1
  244.2 13.2 %collective-permute-done = bf16[512,1024]{1,0:T(8,128)(2,1)S(1)} collective-permute-done((bf16[512,1024]{1,0:T(8,128)(2,1)}, bf16[512,1024]{1,0:T(8,128)(2,1)S(1)}, u32[]{:S(2)}, u32[]{:S(2)}) %collective-permute-start) | collective-permute-done | bytes 1048608 | tf_op jit(solution)/shard_map/ppermute | solution.py:10
  257.4 5.2 %collective-permute-done.1 = bf16[512,1024]{1,0:T(8,128)(2,1)S(1)} collective-permute-done((bf16[512,1024]{1,0:T(8,128)(2,1)S(1)}, bf16[512,1024]{1,0:T(8,128)(2,1)S(1)}, u32[]{:S(2)}, u32[]{:S(2)}) %collective-permute-start.1) | collective-permute-done | bytes 1048608 | tf_op jit(solution)/shard_map/ppermute | solution.py:10
  264.1 3.1 all-reduce.7.cloned.1.call-done
  267.2 89.1 %reduce-scatter.3.cloned.1.call-done = f32[2,32,2048]{2,1,0:T(8,128)} async-done(((f32[2,512,2048]{2,1,0:T(8,128)}), f32[2,32,2048]{2,1,0:T(8,128)}) %reduce-scatter.3.cloned.1.call-update) | async-done | bytes 524304 | tf_op jit(solution)/shard_map/reduce_scatter | solution.py:140
  356.3 88.9 %reduce-scatter.5.cloned.1.call-done = f32[2,128,512]{2,1,0:T(8,128)} async-done(((f32[2,2048,512]{2,1,0:T(8,128)}), f32[2,128,512]{2,1,0:T(8,128)}) %reduce-scatter.5.cloned.1.call-update) | async-done | bytes 524304 | tf_op jit(solution)/shard_map/reduce_scatter | solution.py:141
  (100 shorter events, 25.3 us)
Async XLA Ops:
  7.2 1.6 copy-start
  7.2 1.6 copy-start.1
  8.4 2.6 copy-start.17
  8.8 2.3 copy-start.13
  37.4 1.5 copy-start.24
  39.0 2.0 copy-start.11
  41.0 18.7 %all-to-all-start.3 = ((bf16[1,32,16,1024]{3,2,0,1:T(8,128)(2,1)}), bf16[1,32,16,1024]{3,2,0,1:T(8,128)(2,1)S(1)}, u32[]{:S(2)}, u32[]{:S(2)}) async-start(bf16[1,32,16,1024]{3,2,0,1:T(8,128)(2,1)} %copy.302), calls=%async_computation.3 | async-start | bytes 2097152 | tf_op jit(solution)/shard_map/all_to_all | solution.py:70
  44.7 217.9 %all-reduce.5.cloned.1.call-start = ((), (), s32[]{:S(2)}) async-start(), calls=%async_computation.10 | async-start | bytes 2097152
  46.9 3.1 copy-start.7
  60.2 2.8 copy-start.3
  63.0 4.3 copy-start.22
  66.3 1.0 copy-start.5
  67.4 2.4 copy-start.25
  67.4 2.5 copy-start.29
  69.9 7.2 %copy-start.2 = (f32[2,512,2048]{2,1,0:T(8,128)}, f32[2,512,2048]{2,1,0:T(8,128)S(1)}, u32[]{:S(2)}) copy-start(f32[2,512,2048]{2,1,0:T(8,128)S(1)} %fusion.27) | copy-start | bytes 25165828
  77.1 2.4 copy-start.23
  79.5 1.4 copy-start.19
  83.2 4.2 copy-start.8
  112.9 1.1 copy-start.12
  141.9 125.3 %all-reduce.7.cloned.1.call-start = ((), (), s32[]{:S(2)}) async-start(), calls=%async_computation.11 | async-start | bytes 1572864 | tf_op jit(solution)/shard_map/psum | solution.py:138
  142.0 2.8 copy-start.18
  145.1 1.0 copy-start.15
  146.1 1.3 copy-start.6
  147.4 208.9 %reduce-scatter.3.cloned.1.call-start = ((), (), s32[]{:S(2)}) async-start(), calls=%async_computation.8 | async-start | bytes 8912896 | tf_op jit(solution)/shard_map/reduce_scatter | solution.py:140
  155.3 1.2 copy-start.26
  155.3 289.8 %reduce-scatter.5.cloned.1.call-start = ((), (), s32[]{:S(2)}) async-start(), calls=%async_computation.9 | async-start | bytes 8912896 | tf_op jit(solution)/shard_map/reduce_scatter | solution.py:141
  166.5 1.2 copy-start.10
  166.6 1.5 copy-start.14
  195.2 18.5 %all-to-all-start.1 = ((bf16[1,32,16,1024]{3,2,0,1:T(8,128)(2,1)}), bf16[1,32,16,1024]{3,2,0,1:T(8,128)(2,1)}, u32[]{:S(2)}, u32[]{:S(2)}) async-start(bf16[1,32,16,1024]{3,2,0,1:T(8,128)(2,1)} %copy.285), calls=%async_computation.1 | async-start | bytes 2097152 | tf_op jit(solution)/shard_map/all_to_all | solution.py:70
  201.2 3.1 copy-start.20
  232.5 7.5 %copy-start.16 = (bf16[2,256,1024]{2,1,0:T(8,128)(2,1)S(1)}, bf16[2,256,1024]{2,1,0:T(8,128)(2,1)}, u32[]{:S(2)}) copy-start(bf16[2,256,1024]{2,1,0:T(8,128)(2,1)} %copy-done.15) | copy-start | bytes 3145732
  232.5 8.0 %copy-start.21 = (f32[512,1024]{1,0:T(8,128)S(1)}, f32[512,1024]{1,0:T(8,128)}, u32[]{:S(2)}) copy-start(f32[512,1024]{1,0:T(8,128)} %copy.308) | copy-start | bytes 6291460
  236.3 4.2 copy-start.4
  236.3 4.2 copy-start.9
  236.3 21.1 %collective-permute-start = (bf16[512,1024]{1,0:T(8,128)(2,1)}, bf16[512,1024]{1,0:T(8,128)(2,1)S(1)}, u32[]{:S(2)}, u32[]{:S(2)}) collective-permute-start(bf16[512,1024]{1,0:T(8,128)(2,1)} %add_convert_fusion), channel_id=1, source_target_pairs={{0,32},{32,64},{64,96},{1,33},{33,65},{65,97},{2,34},{34,66},{66,9... | collective-permute-start | bytes 3145736 | tf_op jit(solution)/shard_map/ppermute | solution.py:10
  240.5 2.4 copy-start.30
  241.6 21.0 %collective-permute-start.1 = (bf16[512,1024]{1,0:T(8,128)(2,1)S(1)}, bf16[512,1024]{1,0:T(8,128)(2,1)S(1)}, u32[]{:S(2)}, u32[]{:S(2)}) collective-permute-start(bf16[512,1024]{1,0:T(8,128)(2,1)S(1)} %fusion.35), channel_id=1, source_target_pairs={{32,0},{64,32},{96,64},{33,1},{65,33},{97,65},{34,2},{66,34},{98,6... | collective-permute-start | bytes 3145736 | tf_op jit(solution)/shard_map/ppermute | solution.py:10
  445.1 1.9 copy-start.27
  446.1 1.8 copy-start.28
Sparse Core Ops, SparseCore 0:
  142.1 96.0 all-reduce.4
  241.2 25.9 all-reduce.6
  271.6 84.6 reduce-scatter.2
  360.5 84.5 reduce-scatter.4
where the time goes:
time: 460 us; the launch traced here: 455 us
  waiting for transfers between devices  215 us (47%)
  blocking collectives  79.6 us (17%)
  local copies, waits for them, and re-layouts  62.1 us (14%)
  matrix products  51.9 us (11%)
  other arithmetic  17.6 us (4%)
  between operations  15.1 us (3%)
  starting transfers between devices  13.6 us (3%)
    reduce_scatter x1, waiting for transfers between devices, body(): lax.psum_scatter(up_grad, 'seq', scatter_dimension=1, tiled=True)  89.1 us
    reduce_scatter x1, waiting for transfers between devices, body(): lax.psum_scatter(down_grad, 'seq', scatter_dimension=1, tiled=True)  88.9 us
    all_to_all x2, blocking collectives, run_mixer(): lax.all_to_all(twisted, 'seq', split_axis=2, concat_axis=1, tiled=True)  40.7 us
    all_to_all x1, blocking collectives, body(): lax.all_to_all(d_mixed, 'seq', split_axis=1, concat_axis=0, tiled=True)  20.6 us
    ppermute x2, waiting for transfers between devices, passed_along(): return lax.ppermute(x, axis, pairs)  18.4 us
    all_to_all x1, blocking collectives, body(): lax.all_to_all(d_twisted, 'seq', split_axis=0, concat_axis=1, tiled=True)  18.3 us
    all_to_all x2, waiting for transfers between devices, mix_single(): lax.all_to_all(second_factor(columns, second), 'seq', split_axis=1, conca...  15.8 us
    unnamed x69, local copies, waits for them, and re-layouts  11.7 us
  transfers between devices with their start and end apart: 8, of which 7 were waited for; matrix products, arithmetic and copies ran while one was open for 16% of the time, Pallas kernels for 0%

commit v1 on v0

v1 whole, which is shorter than its diff:
```python
import functools
import math

import jax
import jax.numpy as jnp
from jax import lax
from jax.experimental import pallas as pl
from jax.experimental.pallas import tpu as pltpu
from jax.sharding import PartitionSpec as P

MESH = pl.DeviceIdType.MESH
BF = jnp.bfloat16
F32 = jnp.float32
C0 = math.sqrt(2.0 / math.pi)
C1 = 0.044715

NQ = 16
NS = 4
TOK = 512
HALF = 512
FB = 2048
GRP = 2


def nn(a, b):
    return jnp.dot(a, b, preferred_element_type=F32)


def nt(a, b):
    return lax.dot_general(a, b, (((1,), (1,)), ((), ())), preferred_element_type=F32)


def tn(a, b):
    return lax.dot_general(a, b, (((0,), (0,)), ((), ())), preferred_element_type=F32)


def iota(shape, dim):
    return lax.broadcasted_iota(jnp.int32, shape, dim)


def split(x):
    high = x.astype(BF)
    return high, (x - high.astype(F32)).astype(BF)


def kernel(
    vf_h, vs_h, g_h, f1_h, tw_h, f2_h, up_h, dn_h,
    oact, ograd, oup, odn, otw, ofirst, osecond,
    vs, vf, gg, f1, tw16, f2, up, dn, wmat,
    pin_s, pin_f, pdm, pmx_s, pmx_f, pdi,
    cin_s, cin_f, cdm, cmx_s, cmx_f, cdi,
    twc, hid, direct, act, dl, dh,
    part_up, part_dn, ra_up, ra_dn, rb_up, rb_dn,
    gsum, fg, fg_r, sg, sg_r, outf, dinp, zero, upo, dno, twg, sgo,
    ld, a2s, a2r, rss, rsr, zs, zr, mps, mpr, osem,
):
    sec = lax.axis_index("section")
    me = lax.axis_index("seq")
    core = lax.axis_index("mp")
    y, x = me // 4, me % 4

    def load(src, dst, i):
        copy = pltpu.make_async_copy(src, dst, ld.at[i])
        copy.start()
        return copy

    cols = [pl.ds(0, HALF), pl.ds(HALF, HALF)]
    l_f1 = load(f1_h, f1, 0)
    l_vs = [load(vs_h.at[:, cols[k]], vs.at[k], 1 + k) for k in range(2)]
    l_f2 = load(f2_h, f2, 3)
    own16 = pl.ds(pl.multiple_of(me * 16, 16), 16)
    l_tw = [load(tw_h.at[own16, cols[k]], tw16.at[k], 4 + k) for k in range(2)]
    l_vf = [load(vf_h.at[:, cols[k]], vf.at[k], 6 + k) for k in range(2)]
    l_g = [load(g_h.at[:, cols[k]], gg.at[k], 8 + k) for k in range(2)]
    l_up = [load(up_h.at[k], up.at[k], 10 + k) for k in range(2)]
    l_dn = [load(dn_h.at[k], dn.at[k], 12 + k) for k in range(2)]

    barrier = pltpu.get_barrier_semaphore()

    def peer(d):
        return ((y + d // 4) % 4) * 4 + (x + d % 4) % 4

    def greet(d, carry):
        pl.semaphore_signal(barrier, inc=1, device_id={"seq": peer(d)}, device_id_type=MESH)
        return carry

    lax.fori_loop(1, NQ, greet, 0)
    for by in (1, 3):
        pl.semaphore_signal(
            barrier, inc=1, device_id={"section": (sec + by) % 4}, device_id_type=MESH
        )
    pl.semaphore_signal(barrier, inc=1, device_id={"mp": 1 - core}, device_id_type=MESH)

    def own_rows(ref, k, q):
        return ref.at[k, :, pl.ds(pl.multiple_of(q * 16, 16), 16), :]

    def own_blocks(ref, k, q):
        return ref.at[k, pl.ds(q * 2, 2)]

    def exchange(src_of, dst_of, src, dst, st, k):
        i = 2 * st + k

        def one(d, carry):
            q = peer(d)
            pltpu.make_async_remote_copy(
                src_ref=src_of(src, k, q),
                dst_ref=dst_of(dst, k, me),
                send_sem=a2s.at[i],
                recv_sem=a2r.at[i],
                device_id={"seq": q},
                device_id_type=MESH,
            ).start()
            return carry

        lax.fori_loop(1, NQ, one, 0)
        pltpu.make_async_copy(src_of(src, k, me), dst_of(dst, k, me), a2r.at[i]).start()

    def arrived(dst, st, k):
        pltpu.make_async_copy(dst.at[k], dst.at[k], a2r.at[2 * st + k]).wait()

    def to_columns(src, dst, st, k):
        exchange(own_rows, own_blocks, src, dst, st, k)

    def to_positions(src, dst, st, k):
        exchange(own_blocks, own_rows, src, dst, st, k)

    def first_factor(v, dst, k):
        for a in range(2):
            dst[k, a] = nn(f1[a], v[k, pl.ds(256 * a, 256), :]).astype(BF)

    l_f1.wait()
    l_vs[0].wait()
    first_factor(vs, pin_s, 0)
    pl.semaphore_wait(barrier, NQ + 2)
    to_columns(pin_s, cin_s, 0, 0)
    l_vs[1].wait()
    first_factor(vs, pin_s, 1)
    to_columns(pin_s, cin_s, 0, 1)
    for k in range(2):
        l_vf[k].wait()
        first_factor(vf, pin_f, k)
        to_columns(pin_f, cin_f, 1, k)

    l_f2.wait()
    rows, lanes = iota((512, 512), 0), iota((512, 512), 1)
    swap = jnp.where(lanes == (rows % 16) * 32 + rows // 16, 1.0, 0.0).astype(BF)
    spread = jnp.where(iota((32, 512), 1) // 16 == iota((32, 512), 0), 1.0, 0.0).astype(BF)
    ordered = nn(swap, f2[...]).astype(BF)
    wide = nn(ordered, spread)
    wmat[...] = jnp.where(rows % 16 == lanes % 16, wide, 0.0).astype(BF)
    for k in range(2):
        l_tw[k].wait()

    def twisted(cin, k):
        return (cin[k].astype(F32) * tw16[k].astype(F32)[None]).astype(BF)

    for k in range(2):
        arrived(cin_s, 0, k)
        columns = twisted(cin_s, k)
        twc[k] = columns
        cmx_s[k] = nn(wmat[...], columns.reshape(512, HALF)).astype(BF).reshape(32, 16, HALF)
        to_positions(cmx_s, pmx_s, 2, k)
    for k in range(2):
        arrived(cin_f, 1, k)
        columns = twisted(cin_f, k)
        cmx_f[k] = nn(wmat[...], columns.reshape(512, HALF)).astype(BF).reshape(32, 16, HALF)
        to_positions(cmx_f, pmx_f, 3, k)

    def rs_parts(axis, part, ra, rb):
        mine = x if axis == "x" else y
        other = y if axis == "x" else x
        rows_half = part.shape[2] // 2

        def device(first, by):
            along = (first + by) % 4
            if axis == "x":
                return (y * 4 + along, along * 4 + x)
            return (along * 4 + x, y * 4 + along)

        def piece(phase, by, h):
            if phase == 0:
                return part.at[(mine + by) % 4, pl.ds(2 * h, 2)]
            return part.at[mine, (other + by) % 4, pl.ds(rows_half * h, rows_half)]

        def target(phase, by):
            return device(mine if phase == 0 else other, by)[phase]

        def land(phase, slot):
            return (ra if phase == 0 else rb).at[slot]

        return piece, target, land

    units = []
    for k in range(2):
        units.append(rs_parts("x", part_up.at[k], ra_up.at[k], rb_up.at[k]))
        units.append(rs_parts("y", part_dn.at[k], ra_dn.at[k], rb_dn.at[k]))

    def rs_copy(u, phase, slot, by, h, to):
        piece, target, land = units[u]
        return pltpu.make_async_remote_copy(
            src_ref=piece(phase, by, h),
            dst_ref=land(phase, slot),
            send_sem=rss.at[u, phase * 6 + slot],
            recv_sem=rsr.at[u, phase * 6 + slot],
            device_id={"seq": target(phase, to)},
            device_id_type=MESH,
        )

    SLOTS = ((2, 0, 1), (1, 1, 1), (2, 1, 3), (3, 0, 3), (1, 0, 1), (3, 1, 3))

    def rs_first(u, phase):
        for slot in (0, 2, 1, 3):
            rs_copy(u, phase, slot, *SLOTS[slot]).start()

    def rs_second(u, phase):
        piece, target, land = units[u]
        for slot, after in ((4, 0), (5, 2)):
            by, h, to = SLOTS[slot]
            rs_copy(u, phase, after, *SLOTS[after]).wait_recv()
            ref = piece(phase, by, h)
            ref[...] = (ref[...].astype(F32) + land(phase, after)[...].astype(F32)).astype(BF)
            rs_copy(u, phase, slot, by, h, to).start()

    def rs_third(u, phase, finish):
        piece, target, land = units[u]
        for h, left, right in ((0, 3, 4), (1, 1, 5)):
            for slot in (left, right):
                rs_copy(u, phase, slot, *SLOTS[slot]).wait_recv()
            ref = piece(phase, 0, h)
            total = (
                ref[...].astype(F32)
                + land(phase, left)[...].astype(F32)
                + land(phase, right)[...].astype(F32)
            )
            finish(ref, h, total)

    def keep(ref, h, total):
        ref[...] = total.astype(BF)

    def rs_sent(u):
        for phase in range(2):
            for slot in range(6):
                rs_copy(u, phase, slot, *SLOTS[slot]).wait_send()

    def gated(v, mixed, k, r):
        rs = pl.ds(r * 128, 128)
        values = v[k, rs, :].astype(F32)
        gate = jax.nn.sigmoid(values)
        mix = mixed[k, r // 2, pl.ds(pl.multiple_of((r % 2) * 128, 128), 128), :].astype(F32)
        return rs, values, gate, mix

    def chunk(j):
        return pl.ds(pl.multiple_of(j * 512, 512), 512)

    def channel_saved(k):
        def start(r, carry):
            rs, values, gate, mix = gated(vs, pmx_s, k, r)
            hid[k, rs, :] = (values + mix * gate).astype(BF)
            dh[rs, :] = gg[k, rs, :].astype(F32)
            return carry

        lax.fori_loop(0, 4, start, 0)

        def step(j, carry):
            up_part = up[k, :, chunk(j)]
            u = nn(hid[k], up_part)
            back = nt(gg[k], dn[k, chunk(j), :])
            square = u * u
            th = jnp.tanh(C0 * u * (1.0 + C1 * square))
            lift = 0.5 * (1.0 + th)
            act[j] = (u * lift).astype(BF)
            slope = lift + (0.5 * C0) * u * (1.0 - th * th) * (1.0 + (3.0 * C1) * square)
            d_lift = (back * slope).astype(BF)
            dl[j] = d_lift
            dh[...] += nt(d_lift, up_part)
            return carry

        lax.fori_loop(0, 4, step, 0)

        def end(r, carry):
            rs, values, gate, mix = gated(vs, pmx_s, k, r)
            d_hidden = dh[rs, :]
            pdm[k, r // 2, pl.ds(pl.multiple_of((r % 2) * 128, 128), 128), :] = (
                d_hidden * gate
            ).astype(BF)
            direct[k, rs, :] = d_hidden * (1.0 + mix * gate * (1.0 - gate))
            return carry

        lax.fori_loop(0, 4, end, 0)

    def gradients(k):
        def step_up(j, carry):
            total = tn(hid[k], dl[j]).astype(BF).reshape(4, 4, 32, 512)
            for yy in range(4):
                part_up[k, :, yy, :, chunk(j)] = total[yy]
            return carry

        lax.fori_loop(0, 4, step_up, 0)
        rs_first(2 * k, 0)

        def step_down(j, carry):
            part_dn[k, j] = tn(act[j], gg[k]).astype(BF).reshape(4, 128, 512)
            return carry

        lax.fori_loop(0, 4, step_down, 0)
        rs_first(2 * k + 1, 0)

    for k in range(2):
        l_g[k].wait()
        l_up[k].wait()
        l_dn[k].wait()
        arrived(pmx_s, 2, k)
        channel_saved(k)
        to_columns(pdm, cdm, 4, k)
        gradients(k)

    def columns_back(k):
        arrived(cdm, 4, k)
        grads = cdm[k].reshape(512, HALF)
        d_twisted = tn(wmat[...], grads).astype(BF).astype(F32).reshape(32, 16, HALF)
        cdi[k] = (d_twisted * tw16[k].astype(F32)[None]).astype(BF)
        to_positions(cdi, pdi, 5, k)
        twg[:, cols[k]] = jnp.sum(d_twisted * cin_s[k].astype(F32), axis=0)
        product = nt(grads, twc[k].reshape(512, HALF))
        if k == 0:
            gsum[...] = product
        else:
            gsum[...] += product

    columns_back(0)
    rs_second(0, 0)
    rs_second(1, 0)
    columns_back(1)
    rs_second(2, 0)
    rs_second(3, 0)

    rows2, lanes2 = iota((512, 512), 0), iota((512, 512), 1)
    picked = jnp.where(rows2 % 16 == lanes2 % 16, gsum[...], 0.0)
    gather = jnp.where(iota((512, 32), 0) // 16 == iota((512, 32), 1), 1.0, 0.0).astype(BF)
    high, low = split(picked)
    small = nn(high, gather) + nn(low, gather)
    back_swap = jnp.where(lanes2 == (rows2 % 32) * 16 + rows2 // 32, 1.0, 0.0).astype(BF)
    high, low = split(small)
    sg[...] = nn(back_swap, high) + nn(back_swap, low)

    def mp_copy(src, dst, i):
        return pltpu.make_async_remote_copy(
            src_ref=src,
            dst_ref=dst,
            send_sem=mps.at[i],
            recv_sem=mpr.at[i],
            device_id={"mp": 1 - core},
            device_id_type=MESH,
        )

    mp_copy(sg, sg_r, 0).start()

    def act_copy(k):
        return pltpu.make_async_remote_copy(
            src_ref=outf.at[k],
            dst_ref=oact.at[:, cols[k]],
            send_sem=zs.at[k],
            recv_sem=zr.at[k],
            device_id={"section": (sec + 1) % 4},
            device_id_type=MESH,
        )

    def grad_copy(k):
        return pltpu.make_async_remote_copy(
            src_ref=dinp.at[k],
            dst_ref=ograd.at[:, cols[k]],
            send_sem=zs.at[2 + k],
            recv_sem=zr.at[2 + k],
            device_id={"section": (sec + 3) % 4},
            device_id_type=MESH,
        )

    def channel_fresh(k):
        def start(r, carry):
            rs, values, gate, mix = gated(vf, pmx_f, k, r)
            hidden = (values + mix * gate).astype(BF)
            pmx_f[k, r // 2, pl.ds(pl.multiple_of((r % 2) * 128, 128), 128), :] = hidden
            dh[rs, :] = hidden.astype(F32)
            return carry

        lax.fori_loop(0, 4, start, 0)

        def step(j, carry):
            u = nn(pmx_f[k].reshape(TOK, HALF), up[k, :, chunk(j)])
            th = jnp.tanh(C0 * u * (1.0 + C1 * (u * u)))
            dh[...] += nn((0.5 * u * (1.0 + th)).astype(BF), dn[k, chunk(j), :])
            return carry

        lax.fori_loop(0, 4, step, 0)
        outf[k] = dh[...].astype(BF)

    zero[...] = jnp.zeros_like(zero)

    def blank(dst, k, i):
        return pltpu.make_async_copy(zero, dst.at[:, cols[k]], osem.at[i])

    @pl.when(sec == 0)
    def _():
        for k in range(2):
            blank(oact, k, k).start()

    @pl.when(sec == NS - 1)
    def _():
        for k in range(2):
            blank(ograd, k, k).start()

    for k in range(2):
        arrived(pmx_f, 3, k)
        channel_fresh(k)

        @pl.when(sec < NS - 1)
        def _():
            act_copy(k).start()

        rs_third(2 * k, 0, keep)
        rs_first(2 * k, 1)
        rs_third(2 * k + 1, 0, keep)
        rs_first(2 * k + 1, 1)

    for k in range(2):
        arrived(pdi, 5, k)
        for a in range(2):
            rs = pl.ds(256 * a, 256)
            dinp[k, rs, :] = (direct[k, rs, :] + tn(f1[a], pdi[k, a])).astype(BF)

        @pl.when(sec > 0)
        def _():
            grad_copy(k).start()

        for a in range(2):
            product = nt(pdi[k, a], vs[k, pl.ds(256 * a, 256), :])
            if k == 0:
                fg[a] = product
            else:
                fg[a] += product
    mp_copy(fg, fg_r, 1).start()

    def store(src, dst, i):
        copy = pltpu.make_async_copy(src, dst, osem.at[i])
        copy.start()
        return copy

    stores = [store(twg, otw, 2)]
    mp_copy(sg, sg_r, 0).wait()
    sgo[...] = sg[...] + sg_r[...]
    stores.append(store(sgo, osecond, 3))
    for u in range(4):
        rs_second(u, 1)
    mp_copy(fg, fg_r, 1).wait()
    fg[...] += fg_r[...]
    stores.append(store(fg, ofirst, 4))
    for u in range(4):
        k = u // 2
        out = (upo, dno)[u % 2]
        height = out.shape[1] // 2

        def last(ref, h, total):
            out[k, pl.ds(height * h, height), :] = total

        rs_third(u, 1, last)
        stores.append(store(out.at[k], (oup, odn)[u % 2].at[k], 5 + u))

    for st, (src, kind) in enumerate(
        ((pin_s, 0), (pin_f, 0), (cmx_s, 1), (cmx_f, 1), (pdm, 0), (cdi, 1))
    ):
        for k in range(2):
            ref = src.at[k, :, pl.ds(0, 240), :] if kind == 0 else src.at[k, pl.ds(0, 30)]
            pltpu.make_async_copy(ref, ref, a2s.at[2 * st + k]).wait()
    for u in range(4):
        rs_sent(u)

    @pl.when(sec < NS - 1)
    def _():
        for k in range(2):
            act_copy(k).wait_send()
            grad_copy(k).wait_recv()

    @pl.when(sec > 0)
    def _():
        for k in range(2):
            grad_copy(k).wait_send()
            act_copy(k).wait_recv()

    @pl.when(sec == 0)
    def _():
        for k in range(2):
            blank(oact, k, k).wait()

    @pl.when(sec == NS - 1)
    def _():
        for k in range(2):
            blank(ograd, k, k).wait()

    for copy in stores:
        copy.wait()


def body(fresh, saved, cotangent, factor_one, twiddle, factor_two, up_weight, down_weight):
    any_space = pl.BlockSpec(memory_space=pl.ANY)
    position = pltpu.VMEM((2, 2, 256, HALF), BF)
    column = pltpu.VMEM((2, 32, 16, HALF), BF)
    rows = pltpu.VMEM((2, TOK, HALF), BF)
    dma = pltpu.SemaphoreType.DMA
    outs = pl.pallas_call(
        kernel,
        out_shape=(
            jax.ShapeDtypeStruct((TOK, 1024), BF),
            jax.ShapeDtypeStruct((TOK, 1024), BF),
            jax.ShapeDtypeStruct((2, 32, FB), F32),
            jax.ShapeDtypeStruct((2, 128, 512), F32),
            jax.ShapeDtypeStruct((16, 1024), F32),
            jax.ShapeDtypeStruct((2, 256, 256), F32),
            jax.ShapeDtypeStruct((512, 32), F32),
        ),
        in_specs=[any_space] * 8,
        out_specs=(any_space,) * 7,
        scratch_shapes=[
            rows, rows, rows,
            pltpu.VMEM((2, 256, 256), BF),
            pltpu.VMEM((2, 16, HALF), BF),
            pltpu.VMEM((512, 32), BF),
            pltpu.VMEM((2, 512, FB), BF),
            pltpu.VMEM((2, FB, 512), BF),
            pltpu.VMEM((512, 512), BF),
            position, position, position, position, position, position,
            column, column, column, column, column, column,
            column,
            rows,
            pltpu.VMEM((2, TOK, HALF), F32),
            pltpu.VMEM((4, TOK, 512), BF),
            pltpu.VMEM((4, TOK, 512), BF),
            pltpu.VMEM((TOK, HALF), F32),
            pltpu.VMEM((2, 4, 4, 32, FB), BF),
            pltpu.VMEM((2, 4, 4, 128, 512), BF),
            pltpu.VMEM((2, 6, 2, 32, FB), BF),
            pltpu.VMEM((2, 6, 2, 128, 512), BF),
            pltpu.VMEM((2, 6, 16, FB), BF),
            pltpu.VMEM((2, 6, 64, 512), BF),
            pltpu.VMEM((512, 512), F32),
            pltpu.VMEM((2, 256, 256), F32),
            pltpu.VMEM((2, 256, 256), F32),
            pltpu.VMEM((512, 32), F32),
            pltpu.VMEM((512, 32), F32),
            rows, rows,
            pltpu.VMEM((TOK, HALF), BF),
            pltpu.VMEM((2, 32, FB), F32),
            pltpu.VMEM((2, 128, 512), F32),
            pltpu.VMEM((16, 1024), F32),
            pltpu.VMEM((512, 32), F32),
            dma((14,)), dma((12,)), dma((12,)), dma((4, 12)), dma((4, 12)),
            dma((4,)), dma((4,)), dma((2,)), dma((2,)), dma((9,)),
        ],
        compiler_params=pltpu.CompilerParams(
            collective_id=0, has_side_effects=True, vmem_limit_bytes=63 * 1024 * 1024
        ),
    )(
        fresh[0], saved[0], cotangent[0], factor_one[0], twiddle[0],
        factor_two[0].reshape(512, 32), up_weight[0], down_weight[0],
    )
    act, grad, up_grad, down_grad, twiddle_grad, first_grad, second_grad = outs
    return (
        act[None],
        grad[None],
        up_grad[None],
        down_grad[None],
        twiddle_grad[None],
        first_grad[None],
        second_grad.reshape(1, 16, 32, 32),
    )


def solution(mesh):
    return jax.shard_map(
        body,
        mesh=mesh,
        in_specs=(
            P("section", "seq", "mp"),
            P("section", "seq", "mp"),
            P("section", "seq", "mp"),
            P("section", "seq", None, None),
            P("section", None, "mp"),
            P("section", "seq", None, None),
            P("section", "mp", None, None),
            P("section", "mp", None, None),
        ),
        out_specs=(
            P("section", "seq", "mp"),
            P("section", "seq", "mp"),
            P("section", "mp", "seq", None),
            P("section", "mp", "seq", None),
            P("section", "seq", "mp"),
            P("section", "seq", None, None),
            P("section", "seq", None, None),
        ),
        check_vma=False,
    )
```

time: 460 us -> 145 us (0.32)
  waiting for transfers between devices: 215 us -> 0 us
  Pallas kernels: 0 us -> 135 us
  blocking collectives: 79.6 us -> 0 us
  local copies, waits for them, and re-layouts: 62.1 us -> 8.39 us
  matrix products: 51.9 us -> 0 us
  other arithmetic: 17.6 us -> 0 us
  between operations: 15.1 us -> 0.69 us
  starting transfers between devices: 13.6 us -> 0 us
    reduce_scatter x2 -> x0, waiting for transfers between devices: 178 us -> none  [the longest x1 89.1 us: body(): lax.psum_scatter(up_grad, 'seq', scatter_dimension=1, tiled=True)]
    pallas_call x0 -> x1, Pallas kernels: none -> 135 us  [body(): pl.pallas_call(kernel, out_shape=(jax.ShapeDtypeStruct((TOK, 1024), BF),...]
    all_to_all x4 -> x0, blocking collectives: 79.6 us -> none  [the longest x2 40.7 us: run_mixer(): lax.all_to_all(twisted, 'seq', split_axis=2, concat_axis=1, tiled=True)]
    dot_general x14 -> x0, matrix products: 51.9 us -> none  [the longest x1 11.3 us: channel_forward(): jnp.einsum('tkf,kfd->tkd', activated, down_local, preferred_element_type=...]
    convert_element_type x17 -> x0, local copies, waits for them, and re-layouts: 28.1 us -> none  [the longest x4 9.44 us: channel_forward(): inputs.astype(jnp.float32) + mixed.astype(jnp.float32) * gating]
    ppermute x2 -> x0, waiting for transfers between devices: 18.4 us -> none  [passed_along(): return lax.ppermute(x, axis, pairs)]
    all_to_all x2 -> x0, waiting for transfers between devices: 15.8 us -> none  [mix_single(): lax.all_to_all(second_factor(columns, second), 'seq', split_axis=1, conca...]
    convert_element_type x9 -> x0, other arithmetic: 13.9 us -> none  [the longest x1 3.76 us: channel_forward(): (hidden.astype(jnp.float32) + projected.reshape(tokens, width_local)).ast...]
  transfers between devices with their start and end apart: 8 -> 0, of which waited for: 7 -> 0; matrix products, arithmetic and copies ran while one was open for 16% -> 0% of each run, Pallas kernels for 0% -> 0%
where the time goes in v1:
time: 145 us; the launch traced here: 144 us
  Pallas kernels  135 us (93%)
  local copies, waits for them, and re-layouts  8.39 us (6%)
    pallas_call x1, Pallas kernels, body(): pl.pallas_call(kernel, out_shape=(jax.ShapeDtypeStruct((TOK, 1024), BF),...  135 us
    unnamed x17, local copies, waits for them, and re-layouts  8.39 us

profile of v1, /device:TPU:1, one launch (start us, length us, event | category | flops | bytes accessed | tf_op | source)
XLA Modules:
  0.0 143.8 jit_solution(11940584006316723467)
XLA Ops:
  0.6 134.7 %shard_map.135 = (bf16[512,1024]{1,0:T(8,128)(2,1)}, bf16[512,1024]{1,0:T(8,128)(2,1)}, f32[2,32,2048]{2,1,0:T(8,128)}, f32[2,128,512]{2,1,0:T(8,128)}, f32[16,1...) custom-call(bf16[512,1024]{1,0:T(8,128)(2,1)} %bitcast.17, bf16[512,1024]{1,0:T(8,128)(2,1)} %bitcast.18, ...), custom_call_target="tpu_custom_call" | custom-call | tf_op jit(solution)/shard_map/pallas_call | solution.py:509
  135.3 0.0 copy-start.2
  135.3 0.0 copy-start.1
  135.4 0.0 copy-start.4
  135.4 0.0 copy-start
  135.4 0.0 copy-start.3
  135.4 2.4 %copy.22 = bf16[1,512,1024]{2,1,0:T(8,128)(2,1)} copy(bf16[1,512,1024]{2,1,0:T(8,128)(2,1)} %bitcast.21) | data formatting | bytes 2097152
  137.8 2.3 %copy.23 = bf16[1,512,1024]{2,1,0:T(8,128)(2,1)} copy(bf16[1,512,1024]{2,1,0:T(8,128)(2,1)} %bitcast.20) | data formatting | bytes 2097152
  140.0 0.0 copy-done.2
  140.0 0.8 copy.24
  140.8 0.0 copy-done.1
  140.8 0.8 copy.25
  141.6 0.0 copy-done.4
  141.6 0.6 copy.26
  142.3 0.0 copy-done
  142.3 0.8 copy.27
  143.1 0.0 copy-done.3
  143.1 0.7 copy.28
Async XLA Ops:
  135.3 4.7 %copy-start.2 = (f32[2,32,2048]{2,1,0:T(8,128)S(1)}, f32[2,32,2048]{2,1,0:T(8,128)}, u32[]{:S(2)}) copy-start(f32[2,32,2048]{2,1,0:T(8,128)} %get-tuple-element.16) | copy-start | bytes 1572868
  135.3 5.5 %copy-start.1 = (f32[2,128,512]{2,1,0:T(8,128)S(1)}, f32[2,128,512]{2,1,0:T(8,128)}, u32[]{:S(2)}) copy-start(f32[2,128,512]{2,1,0:T(8,128)} %get-tuple-element.17) | copy-start | bytes 1572868
  135.4 6.3 %copy-start.4 = (f32[16,1024]{1,0:T(8,128)S(1)}, f32[16,1024]{1,0:T(8,128)}, u32[]{:S(2)}) copy-start(f32[16,1024]{1,0:T(8,128)} %get-tuple-element.18) | copy-start | bytes 196612
  135.4 6.9 %copy-start = (f32[2,256,256]{2,1,0:T(8,128)S(1)}, f32[2,256,256]{2,1,0:T(8,128)}, u32[]{:S(2)}) copy-start(f32[2,256,256]{2,1,0:T(8,128)} %get-tuple-element.19) | copy-start | bytes 1572868
  135.4 7.7 %copy-start.3 = (f32[512,32]{1,0:T(8,128)S(1)}, f32[512,32]{1,0:T(8,128)}, u32[]{:S(2)}) copy-start(f32[512,32]{1,0:T(8,128)} %get-tuple-element.20) | copy-start | bytes 196612

commit v2 on v1

v2 whole, which is shorter than its diff:
```python
import math

import jax
import jax.numpy as jnp
from jax import lax
from jax.experimental import pallas as pl
from jax.experimental.pallas import tpu as pltpu
from jax.sharding import PartitionSpec as P

MESH = pl.DeviceIdType.MESH
BF = jnp.bfloat16
F32 = jnp.float32
C0 = math.sqrt(2.0 / math.pi)
C1 = 0.044715

NQ = 16
NS = 4
TOK = 512
HALF = 512
FB = 2048
GRP = 2


def nn(a, b):
    return jnp.dot(a, b, preferred_element_type=F32)


def nt(a, b):
    return lax.dot_general(a, b, (((1,), (1,)), ((), ())), preferred_element_type=F32)


def tn(a, b):
    return lax.dot_general(a, b, (((0,), (0,)), ((), ())), preferred_element_type=F32)


def iota(shape, dim):
    return lax.broadcasted_iota(jnp.int32, shape, dim)


def split(x):
    high = x.astype(BF)
    return high, (x - high.astype(F32)).astype(BF)


def kernel(
    vf_h, vs_h, g_h, f1_h, tw_h, f2_h, up_h, dn_h,
    oact, ograd, oup, odn, otw, ofirst, osecond,
    vs, vf, gg, f1, tw16, tws, f2o, f2c, up, dn, wup, wdn, wmf, wms,
    pin_s, pin_f, pdi, pdr, pmx_f,
    ci, cv, cg, cdi, cdr, cin_f, cmx_f,
    twc, mix, dm, hid, act, dl, dh,
    part, mpb, ra, xsum, wgr,
    fg, fg_r, sgp, sgr, sg, outf, dinp, zero, upo, dno, twg, sgo,
    ld, a2s, a2r, nbs, nbr, rss, rsr, mxs, mxr, xss, xsr, zs, zr, sms, smr, osem,
):
    sec = lax.axis_index("section")
    me = lax.axis_index("seq")
    core = lax.axis_index("mp")
    y, x = me // 4, me % 4
    ks = x % 2
    kc = x // 2
    home = core == kc
    away = core != kc
    base = 64 * y + 32 * core

    def at16(start, size=16):
        return pl.ds(pl.multiple_of(start, 16), size)

    def wide(start):
        return pl.ds(pl.multiple_of(start, 512), 512)

    def load(src, dst, i):
        copy = pltpu.make_async_copy(src, dst, ld.at[i])
        copy.start()
        return copy

    cols = [pl.ds(0, HALF), pl.ds(HALF, HALF)]
    l_f1 = load(f1_h, f1, 0)
    l_vs = [load(vs_h.at[:, :, cols[k]], vs.at[k], 1 + k) for k in range(2)]
    l_g = [load(g_h.at[:, :, cols[k]], gg.at[k], 3 + k) for k in range(2)]
    l_f2 = load(f2_h, f2o, 5)
    l_tw = [load(tw_h.at[at16(me * 16), cols[k]], tw16.at[k], 6 + k) for k in range(2)]
    l_vf = [load(vf_h.at[:, :, cols[k]], vf.at[k], 8 + k) for k in range(2)]
    l_up = [load(up_h.at[k], up.at[k], 10 + k) for k in range(2)]
    l_dn = [load(dn_h.at[k], dn.at[k], 12 + k) for k in range(2)]

    barrier = pltpu.get_barrier_semaphore()

    def peer(d):
        return ((y + d // 4) % 4) * 4 + (x + d % 4) % 4

    def greet(d, carry):
        pl.semaphore_signal(
            barrier,
            inc=1,
            device_id={"seq": peer(d % 16), "mp": (core + d // 16) % 2},
            device_id_type=MESH,
        )
        return carry

    lax.fori_loop(1, 2 * NQ, greet, 0)
    for by in (1, 3):
        pl.semaphore_signal(
            barrier, inc=1, device_id={"section": (sec + by) % 4}, device_id_type=MESH
        )

    def remote(src, dst, send_sem, recv_sem, device):
        return pltpu.make_async_remote_copy(
            src_ref=src,
            dst_ref=dst,
            send_sem=send_sem,
            recv_sem=recv_sem,
            device_id=device,
            device_id_type=MESH,
        )

    def column_piece(src, dst, i, h, d):
        yy = (y + d // 4) % 4
        slot = (x + (d // 2) % 2) % 2
        cc = (core + d % 2) % 2
        return (
            src.at[slot, :, at16(64 * yy + 32 * cc + 16 * h), :],
            dst.at[h, pl.ds(2 * me, 2)],
            {"seq": yy * 4 + 2 * core + slot, "mp": cc},
        )

    def position_piece(src, dst, i, h, d):
        q = peer(d)
        return (
            src.at[h, pl.ds(2 * q, 2)],
            dst.at[ks, :, at16(base + 16 * h), :],
            {"seq": q, "mp": kc},
        )

    def scatter(piece, src, dst, i, h):
        def one(d, carry):
            a, b, device = piece(src, dst, i, h, d)
            remote(a, b, a2s.at[i], a2r.at[i], device).start()
            return carry

        lax.fori_loop(1, NQ, one, 0)
        a, b, device = piece(src, dst, i, h, 0)

        @pl.when(home)
        def _():
            pltpu.make_async_copy(a, b, a2r.at[i]).start()

        @pl.when(away)
        def _():
            remote(a, b, a2s.at[i], a2r.at[i], device).start()

    def fresh_columns(k, q):
        return (
            pin_f.at[k, :, at16(q * 16), :],
            cin_f.at[k, pl.ds(me * 2, 2)],
        )

    def fresh_positions(k, q):
        return (
            cmx_f.at[k, pl.ds(q * 2, 2)],
            pmx_f.at[k, :, at16(me * 16), :],
        )

    def fresh(piece, i, k):
        def one(d, carry):
            q = peer(d)
            remote(*piece(k, q), a2s.at[i], a2r.at[i], {"seq": q}).start()
            return carry

        lax.fori_loop(1, NQ, one, 0)
        a, b = piece(k, me)
        pltpu.make_async_copy(a, b, a2r.at[i]).start()

    def arrived(ref, i):
        pltpu.make_async_copy(ref, ref, a2r.at[i]).wait()

    def first_factor(v, dst, k):
        for a in range(2):
            dst[k, a] = nn(f1[a], v[k, a]).astype(BF)

    l_f1.wait()
    for k in range(2):
        l_vs[k].wait()
        first_factor(vs, pin_s, k)
    for k in range(2):
        l_g[k].wait()
    pl.semaphore_wait(barrier, 2 * NQ + 1)

    scatter(column_piece, pin_s, ci, 0, 0)
    scatter(column_piece, vs, cv, 2, 0)
    scatter(column_piece, gg, cg, 4, 0)

    def fact_copy(by):
        return remote(
            f2_h, f2c.at[ks], nbs.at[by - 1], nbr.at[ks], {"seq": y * 4 + (x + by) % 4}
        )

    def tw_rows(c):
        return tw_h.at[at16(64 * y + 32 * c, 32), wide(512 * ks)]

    partner = {"mp": 1 - core}

    def lent():
        return (
            remote(tw_rows(1 - core), tws, nbs.at[3], nbr.at[2], partner),
            remote(up_h.at[ks], wup, nbs.at[4], nbr.at[3], partner),
            remote(dn_h.at[ks], wdn, nbs.at[5], nbr.at[4], partner),
        )

    @pl.when(home)
    def _():
        pltpu.make_async_copy(f2_h, f2c.at[ks], nbr.at[ks]).start()
        for by in range(1, 4):
            fact_copy(by).start()
        for copy in lent():
            copy.start()
        pltpu.make_async_copy(tw_rows(core), tws, nbr.at[2]).start()
        pltpu.make_async_copy(up_h.at[ks], wup, nbr.at[3]).start()
        pltpu.make_async_copy(dn_h.at[ks], wdn, nbr.at[4]).start()

    scatter(column_piece, pin_s, ci, 1, 1)
    scatter(column_piece, vs, cv, 3, 1)
    scatter(column_piece, gg, cg, 5, 1)

    for k in range(2):
        l_vf[k].wait()
        first_factor(vf, pin_f, k)
        fresh(fresh_columns, 10 + k, k)

    def block_diagonal(f2):
        rows, lanes = iota((512, 512), 0), iota((512, 512), 1)
        swap = jnp.where(lanes == (rows % 16) * 32 + rows // 16, 1.0, 0.0).astype(BF)
        spread = jnp.where(iota((32, 512), 1) // 16 == iota((32, 512), 0), 1.0, 0.0).astype(BF)
        ordered = nn(swap, f2).astype(BF)
        return jnp.where(rows % 16 == lanes % 16, nn(ordered, spread), 0.0).astype(BF)

    def near(ref, i):
        pltpu.make_async_copy(ref, ref, nbr.at[i]).wait()

    l_f2.wait()
    wmf[...] = block_diagonal(f2o[...])
    for h in range(2):
        near(f2c.at[h], h)
        wms[h] = block_diagonal(f2c[h])
    near(tws, 2)
    for k in range(2):
        l_tw[k].wait()

    def small_copy(h, cc):
        return remote(
            sgp.at[h],
            sgr.at[x],
            sms.at[2 * h + cc],
            smr.at[x],
            {"seq": y * 4 + 2 * core + h, "mp": cc},
        )

    def twiddle_copy(h):
        return remote(
            twg.at[h],
            otw.at[:, wide(512 * ks)],
            sms.at[4 + h],
            smr.at[4 + ks],
            {"seq": y * 4 + 2 * core + h, "mp": kc},
        )

    def small_each(h, is_self, is_other):
        here = 2 * core + h == x
        for cc in range(2):
            same = jnp.logical_and(here, core == cc)

            if is_self:

                @pl.when(same)
                def _():
                    is_self(pltpu.make_async_copy(sgp.at[h], sgr.at[x], smr.at[x]))

            @pl.when(jnp.logical_not(same))
            def _():
                is_other(small_copy(h, cc))

        same = jnp.logical_and(here, home)

        if is_self:

            @pl.when(same)
            def _():
                is_self(
                    pltpu.make_async_copy(
                        twg.at[h], otw.at[:, wide(512 * ks)], smr.at[4 + ks]
                    )
                )

        @pl.when(jnp.logical_not(same))
        def _():
            is_other(twiddle_copy(h))

    def chunk(j):
        return pl.ds(pl.multiple_of(j * 512, 512), 512)

    def saved(h):
        tw = tws[pl.ds(16 * h, 16), :].astype(F32)[None]
        arrived(ci.at[h], h)
        columns = (ci[h].astype(F32) * tw).astype(BF)
        twc[h] = columns
        mix[...] = nn(wms[h], columns.reshape(512, HALF)).astype(BF).reshape(32, 16, HALF)
        arrived(cv.at[h], 2 + h)
        arrived(cg.at[h], 4 + h)
        top = 512 * h

        def gated(r):
            blocks = pl.ds(r * 8, 8)
            values = cv[h, blocks].reshape(128, HALF).astype(F32)
            mixed = mix[blocks].reshape(128, HALF).astype(F32)
            return blocks, values, jax.nn.sigmoid(values), mixed

        def start(r, carry):
            blocks, values, gate, mixed = gated(r)
            hid[pl.ds(pl.multiple_of(top + r * 128, 128), 128), :] = (
                values + mixed * gate
            ).astype(BF)
            dh[pl.ds(pl.multiple_of(r * 128, 128), 128), :] = (
                cg[h, blocks].reshape(128, HALF).astype(F32)
            )
            return carry

        lax.fori_loop(0, 4, start, 0)
        if h == 0:
            near(wup, 3)
            near(wdn, 4)

        def step(j, carry):
            up_part = wup[:, chunk(j)]
            u = nn(hid[pl.ds(top, 512), :], up_part)
            back = nt(cg[h].reshape(512, HALF), wdn[chunk(j), :])
            square = u * u
            th = jnp.tanh(C0 * u * (1.0 + C1 * square))
            lift = 0.5 * (1.0 + th)
            act[j, pl.ds(top, 512), :] = (u * lift).astype(BF)
            slope = lift + (0.5 * C0) * u * (1.0 - th * th) * (1.0 + (3.0 * C1) * square)
            d_lift = (back * slope).astype(BF)
            dl[j, pl.ds(top, 512), :] = d_lift
            dh[...] += nt(d_lift, up_part)
            return carry

        lax.fori_loop(0, 4, step, 0)

        def end(r, carry):
            blocks, values, gate, mixed = gated(r)
            rs = pl.ds(pl.multiple_of(r * 128, 128), 128)
            d_hidden = dh[rs, :]
            dm[rs, :] = (d_hidden * gate).astype(BF)
            cdr[h, blocks] = (
                (d_hidden * (1.0 + mixed * gate * (1.0 - gate))).astype(BF).reshape(8, 16, HALF)
            )
            return carry

        lax.fori_loop(0, 4, end, 0)
        scatter(position_piece, cdr, pdr, 8 + h, h)
        d_twisted = tn(wms[h], dm[...]).astype(BF).astype(F32).reshape(32, 16, HALF)
        cdi[h] = (d_twisted * tw).astype(BF)
        scatter(position_piece, cdi, pdi, 6 + h, h)
        twg[h] = jnp.sum(d_twisted * ci[h].astype(F32), axis=0)

        rows, lanes = iota((512, 512), 0), iota((512, 512), 1)
        product = nt(dm[...], twc[h].reshape(512, HALF))
        high, low = split(jnp.where(rows % 16 == lanes % 16, product, 0.0))
        packed = jnp.zeros((128, 128), F32)
        for group in range(4):
            gather = jnp.where(
                iota((512, 128), 1) == 32 * group + iota((512, 128), 0) // 16, 1.0, 0.0
            ).astype(BF)
            some = slice(128 * group, 128 * group + 128)
            packed = packed + nn(high[some], gather) + nn(low[some], gather)
        sgp[h] = packed
        small_each(h, lambda copy: copy.start(), lambda copy: copy.start())

    for h in range(2):
        saved(h)

    for k in range(2):
        arrived(cin_f.at[k], 10 + k)
        columns = (cin_f[k].astype(F32) * tw16[k].astype(F32)[None]).astype(BF)
        cmx_f[k] = nn(wmf[...], columns.reshape(512, HALF)).astype(BF).reshape(32, 16, HALF)
        fresh(fresh_positions, 12 + k, k)

    def step_up(j, carry):
        total = tn(hid[...], dl[j]).astype(BF).reshape(4, 4, 32, 512)
        part[0, :, :, pl.ds(pl.multiple_of(j * 32, 32), 32), :] = total
        return carry

    lax.fori_loop(0, 4, step_up, 0)

    def step_down(j, carry):
        part[1, j] = tn(act[j], cg[...].reshape(1024, HALF)).astype(BF).reshape(4, 128, 512)
        return carry

    lax.fori_loop(0, 4, step_down, 0)

    def core_copy(t):
        return remote(
            part.at[1 - core, (y + t) % 4], mpb.at[t], mxs.at[t], mxr.at[t], partner
        )

    ORDER = (2, 1, 3, 0)
    for t in ORDER:
        core_copy(t).start()

    SLOTS = ((2, 0, 1), (1, 1, 1), (2, 1, 3), (3, 0, 3), (1, 0, 1), (3, 1, 3))

    def piece(by, h):
        return part.at[core, (y + by) % 4, pl.ds(2 * h, 2)]

    def rs_copy(slot):
        by, h, to = SLOTS[slot]
        return remote(
            piece(by, h),
            ra.at[slot],
            rss.at[slot],
            rsr.at[slot],
            {"seq": ((y + to) % 4) * 4 + x},
        )

    def both(t):
        core_copy(t).wait_recv()
        ref = part.at[core, (y + t) % 4]
        ref[...] = (ref[...].astype(F32) + mpb[t].astype(F32)).astype(BF)

    both(2)
    rs_copy(0).start()
    rs_copy(2).start()
    both(1)
    rs_copy(1).start()
    both(3)
    rs_copy(3).start()
    both(0)

    def rs_second():
        for slot, after in ((4, 0), (5, 2)):
            by, h, to = SLOTS[slot]
            rs_copy(after).wait_recv()
            ref = piece(by, h)
            ref[...] = (ref[...].astype(F32) + ra[after].astype(F32)).astype(BF)
            rs_copy(slot).start()

    def spread_copy(xx):
        return remote(
            xsum.at[xx],
            wgr.at[core, ks],
            xss.at[xx],
            xsr.at[core, ks],
            {"seq": y * 4 + xx, "mp": kc},
        )

    def spread_each(xx, is_self, is_other):
        same = jnp.logical_and(x == xx, home)

        if is_self:

            @pl.when(same)
            def _():
                is_self(
                    pltpu.make_async_copy(xsum.at[xx], wgr.at[core, ks], xsr.at[core, ks])
                )

        @pl.when(jnp.logical_not(same))
        def _():
            is_other(spread_copy(xx))

    def rs_third():
        for h, left, right in ((0, 3, 4), (1, 1, 5)):
            for slot in (left, right):
                rs_copy(slot).wait_recv()
            xsum[pl.ds(2 * h, 2)] = (
                piece(0, h)[...].astype(F32) + ra[left].astype(F32) + ra[right].astype(F32)
            ).astype(BF)
            for xx in (2 * h, 2 * h + 1):
                spread_each(xx, lambda copy: copy.start(), lambda copy: copy.start())

    def act_copy(k):
        return remote(
            outf.at[k],
            oact.at[:, cols[k]],
            zs.at[k],
            zr.at[k],
            {"section": (sec + 1) % 4},
        )

    def grad_copy(k):
        return remote(
            dinp.at[k],
            ograd.at[:, cols[k]],
            zs.at[2 + k],
            zr.at[2 + k],
            {"section": (sec + 3) % 4},
        )

    def channel_fresh(k):
        def start(r, carry):
            rs = pl.ds(pl.multiple_of((r % 2) * 128, 128), 128)
            values = vf[k, r // 2, rs, :].astype(F32)
            mixed = pmx_f[k, r // 2, rs, :].astype(F32)
            hidden = (values + mixed * jax.nn.sigmoid(values)).astype(BF)
            pmx_f[k, r // 2, rs, :] = hidden
            dh[pl.ds(pl.multiple_of(r * 128, 128), 128), :] = hidden.astype(F32)
            return carry

        lax.fori_loop(0, 4, start, 0)

        def step(j, carry):
            u = nn(pmx_f[k].reshape(TOK, HALF), up[k, :, chunk(j)])
            th = jnp.tanh(C0 * u * (1.0 + C1 * (u * u)))
            dh[...] += nn((0.5 * u * (1.0 + th)).astype(BF), dn[k, chunk(j), :])
            return carry

        lax.fori_loop(0, 4, step, 0)
        outf[k] = dh[...].astype(BF)

    zero[...] = jnp.zeros_like(zero)

    def blank(dst, k, i):
        return pltpu.make_async_copy(zero, dst.at[:, cols[k]], osem.at[i])

    @pl.when(sec == 0)
    def _():
        for k in range(2):
            blank(oact, k, k).start()

    @pl.when(sec == NS - 1)
    def _():
        for k in range(2):
            blank(ograd, k, k).start()

    for k in range(2):
        l_up[k].wait()
        l_dn[k].wait()
        arrived(pmx_f.at[k], 12 + k)
        channel_fresh(k)

        @pl.when(sec < NS - 1)
        def _():
            act_copy(k).start()

        if k == 0:
            rs_second()

    for h in range(2):
        arrived(pdr.at[0], 8 + h)
        arrived(pdi.at[0], 6 + h)
    for k in range(2):
        for a in range(2):
            dinp[k, pl.ds(256 * a, 256), :] = (
                pdr[k, a].astype(F32) + tn(f1[a], pdi[k, a])
            ).astype(BF)

        @pl.when(sec > 0)
        def _():
            grad_copy(k).start()

    rs_third()
    for a in range(2):
        fg[a] = nt(pdi[0, a], vs[0, a]) + nt(pdi[1, a], vs[1, a])
    first_copy = remote(fg, fg_r, mxs.at[4], mxr.at[4], partner)
    first_copy.start()

    def store(src, dst, i):
        copy = pltpu.make_async_copy(src, dst, osem.at[i])
        copy.start()
        return copy

    for k in range(4):
        pltpu.make_async_copy(sgr.at[k], sgr.at[k], smr.at[k]).wait()
    packed = (sgr[0] + sgr[1]) + (sgr[2] + sgr[3])
    high, low = split(packed)
    for group in range(4):
        pick = jnp.where(iota((128, 32), 0) == 32 * group + iota((128, 32), 1), 1.0, 0.0).astype(
            BF
        )
        sg[pl.ds(128 * group, 128), :] = nn(high, pick) + nn(low, pick)
    rows, lanes = iota((512, 512), 0), iota((512, 512), 1)
    back_swap = jnp.where(lanes == (rows % 32) * 16 + rows // 32, 1.0, 0.0).astype(BF)
    high, low = split(sg[...])
    sgo[...] = nn(back_swap, high) + nn(back_swap, low)
    stores = [store(sgo, osecond, 2)]
    first_copy.wait()
    fg[...] += fg_r[...]
    stores.append(store(fg, ofirst, 3))
    for slot in range(2):
        for kind in range(2):
            pltpu.make_async_copy(
                wgr.at[kind, slot], wgr.at[kind, slot], xsr.at[kind, slot]
            ).wait()
        for j in range(4):
            upo[slot, :, pl.ds(512 * j, 512)] = wgr[0, slot, pl.ds(32 * j, 32), :].astype(F32)
        dno[slot] = wgr[1, slot].astype(F32)
        stores.append(store(upo.at[slot], oup.at[slot], 4 + slot))
        stores.append(store(dno.at[slot], odn.at[slot], 6 + slot))

    sent = ((pin_s, 0, 0), (vs, 2, 0), (gg, 4, 0), (cdi, 6, 1), (cdr, 8, 1), (pin_f, 10, 0), (cmx_f, 12, 1))
    for src, i, kind in sent:
        for k in range(2):
            most = src.at[k, :, pl.ds(0, 240), :] if kind == 0 else src.at[k, pl.ds(0, 30)]
            pltpu.make_async_copy(most, most, a2s.at[i + k]).wait()
            if i < 10:
                rest = src.at[k, :, pl.ds(0, 16), :] if kind == 0 else src.at[k, pl.ds(0, 2)]

                @pl.when(away)
                def _():
                    pltpu.make_async_copy(rest, rest, a2s.at[i + k]).wait()

    @pl.when(home)
    def _():
        for by in range(1, 4):
            fact_copy(by).wait_send()
        for copy in lent():
            copy.wait_send()

    for h in range(2):
        small_each(h, None, lambda copy: copy.wait_send())
    for slot in range(2):
        otw_part = otw.at[:, cols[slot]]
        pltpu.make_async_copy(otw_part, otw_part, smr.at[4 + slot]).wait()
    for t in range(4):
        core_copy(t).wait_send()
    for slot in range(6):
        rs_copy(slot).wait_send()
    for xx in range(4):
        spread_each(xx, None, lambda copy: copy.wait_send())

    @pl.when(sec < NS - 1)
    def _():
        for k in range(2):
            act_copy(k).wait_send()
            grad_copy(k).wait_recv()

    @pl.when(sec > 0)
    def _():
        for k in range(2):
            grad_copy(k).wait_send()
            act_copy(k).wait_recv()

    @pl.when(sec == 0)
    def _():
        for k in range(2):
            blank(oact, k, k).wait()

    @pl.when(sec == NS - 1)
    def _():
        for k in range(2):
            blank(ograd, k, k).wait()

    for copy in stores:
        copy.wait()


def hand_on(*refs):
    count = (len(refs) - 1) // 3
    sems = refs[-1]
    into = [
        pltpu.make_async_copy(refs[i], refs[2 * count + i], sems.at[0, i]) for i in range(count)
    ]
    out = [
        pltpu.make_async_copy(refs[2 * count + i], refs[count + i], sems.at[1, i])
        for i in range(count)
    ]
    for copy in into:
        copy.start()
    for i in range(count):
        into[i].wait()
        out[i].start()
    for copy in out:
        copy.wait()


def body(fresh, saved, cotangent, factor_one, twiddle, factor_two, up_weight, down_weight):
    any_space = pl.BlockSpec(memory_space=pl.ANY)
    position = pltpu.VMEM((2, 2, 256, HALF), BF)
    column = pltpu.VMEM((2, 32, 16, HALF), BF)
    rows = pltpu.VMEM((2, TOK, HALF), BF)
    square = pltpu.VMEM((512, 512), BF)
    fact = pltpu.VMEM((512, 32), BF)
    dma = pltpu.SemaphoreType.DMA
    shapes = (
        jax.ShapeDtypeStruct((TOK, 1024), BF),
        jax.ShapeDtypeStruct((TOK, 1024), BF),
        jax.ShapeDtypeStruct((2, 32, FB), F32),
        jax.ShapeDtypeStruct((2, 128, 512), F32),
        jax.ShapeDtypeStruct((16, 1024), F32),
        jax.ShapeDtypeStruct((2, 256, 256), F32),
        jax.ShapeDtypeStruct((512, 32), F32),
    )
    outs = pl.pallas_call(
        kernel,
        out_shape=shapes,
        in_specs=[any_space] * 8,
        out_specs=(any_space,) * 7,
        scratch_shapes=[
            position, position, position,
            pltpu.VMEM((2, 256, 256), BF),
            pltpu.VMEM((2, 16, HALF), BF),
            pltpu.VMEM((32, HALF), BF),
            fact,
            pltpu.VMEM((2, 512, 32), BF),
            pltpu.VMEM((2, 512, FB), BF),
            pltpu.VMEM((2, FB, 512), BF),
            pltpu.VMEM((512, FB), BF),
            pltpu.VMEM((FB, 512), BF),
            square,
            pltpu.VMEM((2, 512, 512), BF),
            position, position, position, position, position,
            column, column, column, column, column, column, column,
            column,
            pltpu.VMEM((32, 16, HALF), BF),
            square,
            pltpu.VMEM((2 * TOK, HALF), BF),
            pltpu.VMEM((4, 2 * TOK, 512), BF),
            pltpu.VMEM((4, 2 * TOK, 512), BF),
            pltpu.VMEM((TOK, HALF), F32),
            pltpu.VMEM((2, 4, 4, 128, 512), BF),
            pltpu.VMEM((4, 4, 128, 512), BF),
            pltpu.VMEM((6, 2, 128, 512), BF),
            pltpu.VMEM((4, 128, 512), BF),
            pltpu.VMEM((2, 2, 128, 512), BF),
            pltpu.VMEM((2, 256, 256), F32),
            pltpu.VMEM((2, 256, 256), F32),
            pltpu.VMEM((2, 128, 128), F32),
            pltpu.VMEM((4, 128, 128), F32),
            pltpu.VMEM((512, 32), F32),
            rows, rows,
            pltpu.VMEM((TOK, HALF), BF),
            pltpu.VMEM((2, 32, FB), F32),
            pltpu.VMEM((2, 128, 512), F32),
            pltpu.VMEM((2, 16, HALF), F32),
            pltpu.VMEM((512, 32), F32),
            dma((14,)), dma((14,)), dma((14,)), dma((6,)), dma((5,)), dma((6,)), dma((6,)),
            dma((5,)), dma((5,)), dma((4,)), dma((2, 2)), dma((4,)), dma((4,)),
            dma((6,)), dma((6,)), dma((8,)),
        ],
        compiler_params=pltpu.CompilerParams(
            collective_id=0, has_side_effects=True, vmem_limit_bytes=63 * 1024 * 1024
        ),
    )(
        fresh.reshape(2, 256, 1024), saved.reshape(2, 256, 1024), cotangent.reshape(2, 256, 1024),
        factor_one[0], twiddle[0], factor_two[0].reshape(512, 32), up_weight[0], down_weight[0],
    )
    act, grad, up_grad, down_grad, twiddle_grad, first_grad, second_grad = pl.pallas_call(
        hand_on,
        out_shape=shapes,
        in_specs=[any_space] * 7,
        out_specs=(any_space,) * 7,
        scratch_shapes=[pltpu.VMEM(part.shape, part.dtype) for part in shapes] + [dma((2, 7))],
    )(*outs)
    return (
        act[None],
        grad[None],
        up_grad[None],
        down_grad[None],
        twiddle_grad[None],
        first_grad[None],
        second_grad.reshape(1, 16, 32, 32),
    )


def solution(mesh):
    return jax.shard_map(
        body,
        mesh=mesh,
        in_specs=(
            P("section", "seq", "mp"),
            P("section", "seq", "mp"),
            P("section", "seq", "mp"),
            P("section", "seq", None, None),
            P("section", None, "mp"),
            P("section", "seq", None, None),
            P("section", "mp", None, None),
            P("section", "mp", None, None),
        ),
        out_specs=(
            P("section", "seq", "mp"),
            P("section", "seq", "mp"),
            P("section", "mp", "seq", None),
            P("section", "mp", "seq", None),
            P("section", "seq", "mp"),
            P("section", "seq", None, None),
            P("section", "seq", None, None),
        ),
        check_vma=False,
    )
```

time: 145 us -> 132 us (0.910)
  local copies, waits for them, and re-layouts: 8.39 us -> 0 us
  Pallas kernels: 135 us -> 131 us
    unnamed x17 -> x0, local copies, waits for them, and re-layouts: 8.39 us -> none
    pallas_call x1 -> x2, Pallas kernels: 135 us -> 131 us  [the longest x1 128 us: body(): pl.pallas_call(kernel, out_shape=shapes, in_specs=[any_space] * 8, out_sp...]
where the time goes in v2:
time: 132 us
  Pallas kernels  131 us (99%)
    pallas_call x1, Pallas kernels, body(): pl.pallas_call(kernel, out_shape=shapes, in_specs=[any_space] * 8, out_sp...  128 us
    pallas_call x1, Pallas kernels, body(): pl.pallas_call(hand_on, out_shape=shapes, in_specs=[any_space] * 7, out_s...  3.28 us

profile of v2, /device:TPU:1, one launch (start us, length us, event | category | flops | bytes accessed | tf_op | source)
XLA Modules:
  0.0 132.1 jit_solution(3165632870542921300)
XLA Ops:
  0.6 128.0 %shard_map.135 = (bf16[512,1024]{1,0:T(8,128)(2,1)}, bf16[512,1024]{1,0:T(8,128)(2,1)}, f32[2,32,2048]{2,1,0:T(8,128)}, f32[2,128,512]{2,1,0:T(8,128)}, f32[16,1...) custom-call(bf16[2,256,1024]{2,1,0:T(8,128)(2,1)} %bitcast.17, bf16[2,256,1024]{2,1,0:T(8,128)(2,1)} %bitcast.18, ...), custom_call_target="tpu_custom_call" | custom-call | tf_op jit(solution)/shard_map/pallas_call | solution.py:692
  128.7 3.3 %shard_map.136 = (bf16[512,1024]{1,0:T(8,128)(2,1)}, bf16[512,1024]{1,0:T(8,128)(2,1)}, f32[2,32,2048]{2,1,0:T(8,128)}, f32[2,128,512]{2,1,0:T(8,128)}, f32[16,1...) custom-call(bf16[512,1024]{1,0:T(8,128)(2,1)} %get-tuple-element.21.refs_0_, ...), custom_call_target="tpu_custom_call" | custom-call | tf_op jit(solution)/shard_map/pallas_call | solution.py:746

commit v3 on v2

--- a/solution.py
+++ b/solution.py
@@ -127,8 +127,8 @@
     def position_piece(src, dst, i, h, d):
         q = peer(d)
         return (
-            src.at[h, pl.ds(2 * q, 2)],
-            dst.at[ks, :, at16(base + 16 * h), :],
+            src.at[h, 2 * q + i % 2],
+            dst.at[ks, i % 2, at16(base + 16 * h), :],
             {"seq": q, "mp": kc},
         )
 
@@ -178,17 +178,32 @@
         for a in range(2):
             dst[k, a] = nn(f1[a], v[k, a]).astype(BF)
 
-    l_f1.wait()
-    for k in range(2):
-        l_vs[k].wait()
-        first_factor(vs, pin_s, k)
-    for k in range(2):
-        l_g[k].wait()
-    pl.semaphore_wait(barrier, 2 * NQ + 1)
-
-    scatter(column_piece, pin_s, ci, 0, 0)
-    scatter(column_piece, vs, cv, 2, 0)
-    scatter(column_piece, gg, cg, 4, 0)
+    def send_v(h):
+        if h == 0:
+            for k in range(2):
+                l_vs[k].wait()
+        scatter(column_piece, vs, cv, 2 + h, h)
+
+    def send_g(h):
+        if h == 0:
+            for k in range(2):
+                l_g[k].wait()
+        scatter(column_piece, gg, cg, 4 + h, h)
+
+    def send_inner(h):
+        scatter(column_piece, pin_s, ci, h, h)
+
+    def send_fresh(k):
+        fresh(fresh_columns, 10 + k, k)
+
+    def factor_saved():
+        l_f1.wait()
+        for k in range(2):
+            first_factor(vs, pin_s, k)
+
+    def factor_fresh(k):
+        l_vf[k].wait()
+        first_factor(vf, pin_f, k)
 
     def fact_copy(by):
         return remote(
@@ -207,25 +222,17 @@
             remote(dn_h.at[ks], wdn, nbs.at[5], nbr.at[4], partner),
         )
 
-    @pl.when(home)
-    def _():
-        pltpu.make_async_copy(f2_h, f2c.at[ks], nbr.at[ks]).start()
-        for by in range(1, 4):
-            fact_copy(by).start()
-        for copy in lent():
-            copy.start()
-        pltpu.make_async_copy(tw_rows(core), tws, nbr.at[2]).start()
-        pltpu.make_async_copy(up_h.at[ks], wup, nbr.at[3]).start()
-        pltpu.make_async_copy(dn_h.at[ks], wdn, nbr.at[4]).start()
-
-    scatter(column_piece, pin_s, ci, 1, 1)
-    scatter(column_piece, vs, cv, 3, 1)
-    scatter(column_piece, gg, cg, 5, 1)
-
-    for k in range(2):
-        l_vf[k].wait()
-        first_factor(vf, pin_f, k)
-        fresh(fresh_columns, 10 + k, k)
+    def lend():
+        @pl.when(home)
+        def _():
+            pltpu.make_async_copy(f2_h, f2c.at[ks], nbr.at[ks]).start()
+            for by in range(1, 4):
+                fact_copy(by).start()
+            for copy in lent():
+                copy.start()
+            pltpu.make_async_copy(tw_rows(core), tws, nbr.at[2]).start()
+            pltpu.make_async_copy(up_h.at[ks], wup, nbr.at[3]).start()
+            pltpu.make_async_copy(dn_h.at[ks], wdn, nbr.at[4]).start()
 
     def block_diagonal(f2):
         rows, lanes = iota((512, 512), 0), iota((512, 512), 1)
@@ -237,14 +244,17 @@
     def near(ref, i):
         pltpu.make_async_copy(ref, ref, nbr.at[i]).wait()
 
-    l_f2.wait()
-    wmf[...] = block_diagonal(f2o[...])
-    for h in range(2):
-        near(f2c.at[h], h)
-        wms[h] = block_diagonal(f2c[h])
-    near(tws, 2)
-    for k in range(2):
-        l_tw[k].wait()
+    def fact_fresh():
+        l_f2.wait()
+        wmf[...] = block_diagonal(f2o[...])
+        for k in range(2):
+            l_tw[k].wait()
+
+    def fact_saved():
+        for h in range(2):
+            near(f2c.at[h], h)
+            wms[h] = block_diagonal(f2c[h])
+        near(tws, 2)
 
     def small_copy(h, cc):
         return remote(
@@ -298,14 +308,18 @@
     def chunk(j):
         return pl.ds(pl.multiple_of(j * 512, 512), 512)
 
-    def saved(h):
+    def saved(h, mid=None, after=None):
         tw = tws[pl.ds(16 * h, 16), :].astype(F32)[None]
         arrived(ci.at[h], h)
         columns = (ci[h].astype(F32) * tw).astype(BF)
         twc[h] = columns
         mix[...] = nn(wms[h], columns.reshape(512, HALF)).astype(BF).reshape(32, 16, HALF)
+        if mid:
+            mid()
         arrived(cv.at[h], 2 + h)
         arrived(cg.at[h], 4 + h)
+        if after:
+            after()
         top = 512 * h
 
         def gated(r):
@@ -356,10 +370,11 @@
             return carry
 
         lax.fori_loop(0, 4, end, 0)
-        scatter(position_piece, cdr, pdr, 8 + h, h)
         d_twisted = tn(wms[h], dm[...]).astype(BF).astype(F32).reshape(32, 16, HALF)
         cdi[h] = (d_twisted * tw).astype(BF)
-        scatter(position_piece, cdi, pdi, 6 + h, h)
+        for a in range(2):
+            scatter(position_piece, cdi, pdi, 6 + a, h)
+            scatter(position_piece, cdr, pdr, 8 + a, h)
         twg[h] = jnp.sum(d_twisted * ci[h].astype(F32), axis=0)
 
         rows, lanes = iota((512, 512), 0), iota((512, 512), 1)
@@ -375,36 +390,35 @@
         sgp[h] = packed
         small_each(h, lambda copy: copy.start(), lambda copy: copy.start())
 
-    for h in range(2):
-        saved(h)
-
-    for k in range(2):
+    def second_fresh(k):
         arrived(cin_f.at[k], 10 + k)
         columns = (cin_f[k].astype(F32) * tw16[k].astype(F32)[None]).astype(BF)
         cmx_f[k] = nn(wmf[...], columns.reshape(512, HALF)).astype(BF).reshape(32, 16, HALF)
         fresh(fresh_positions, 12 + k, k)
 
-    def step_up(j, carry):
-        total = tn(hid[...], dl[j]).astype(BF).reshape(4, 4, 32, 512)
-        part[0, :, :, pl.ds(pl.multiple_of(j * 32, 32), 32), :] = total
-        return carry
-
-    lax.fori_loop(0, 4, step_up, 0)
-
-    def step_down(j, carry):
-        part[1, j] = tn(act[j], cg[...].reshape(1024, HALF)).astype(BF).reshape(4, 128, 512)
-        return carry
-
-    lax.fori_loop(0, 4, step_down, 0)
+    def gradients():
+        def step_up(j, carry):
+            total = tn(hid[...], dl[j]).astype(BF).reshape(4, 4, 32, 512)
+            part[0, :, :, pl.ds(pl.multiple_of(j * 32, 32), 32), :] = total
+            return carry
+
+        lax.fori_loop(0, 4, step_up, 0)
+
+        def step_down(j, carry):
+            part[1, j] = tn(act[j], cg[...].reshape(1024, HALF)).astype(BF).reshape(4, 128, 512)
+            return carry
+
+        lax.fori_loop(0, 4, step_down, 0)
+
+        for t in ORDER:
+            core_copy(t).start()
+
+    ORDER = (2, 1, 3, 0)
 
     def core_copy(t):
         return remote(
             part.at[1 - core, (y + t) % 4], mpb.at[t], mxs.at[t], mxr.at[t], partner
         )
-
-    ORDER = (2, 1, 3, 0)
-    for t in ORDER:
-        core_copy(t).start()
 
     SLOTS = ((2, 0, 1), (1, 1, 1), (2, 1, 3), (3, 0, 3), (1, 0, 1), (3, 1, 3))
 
@@ -426,14 +440,13 @@
         ref = part.at[core, (y + t) % 4]
         ref[...] = (ref[...].astype(F32) + mpb[t].astype(F32)).astype(BF)
 
-    both(2)
-    rs_copy(0).start()
-    rs_copy(2).start()
-    both(1)
-    rs_copy(1).start()
-    both(3)
-    rs_copy(3).start()
-    both(0)
+    def core_sums():
+        for t in ORDER:
+            both(t)
+
+    def rs_first():
+        for slot in (0, 2, 1, 3):
+            rs_copy(slot).start()
 
     def rs_second():
         for slot, after in ((4, 0), (5, 2)):
@@ -486,12 +499,13 @@
             {"section": (sec + 1) % 4},
         )
 
-    def grad_copy(k):
+    def grad_copy(k, a):
+        half = pl.ds(256 * a, 256)
         return remote(
-            dinp.at[k],
-            ograd.at[:, cols[k]],
-            zs.at[2 + k],
-            zr.at[2 + k],
+            dinp.at[k, half],
+            ograd.at[half, cols[k]],
+            zs.at[2 + 2 * a + k],
+            zr.at[2 + 2 * a + k],
             {"section": (sec + 3) % 4},
         )
 
@@ -531,7 +545,7 @@
         for k in range(2):
             blank(ograd, k, k).start()
 
-    for k in range(2):
+    def mix_fresh(k):
         l_up[k].wait()
         l_dn[k].wait()
         arrived(pmx_f.at[k], 12 + k)
@@ -541,23 +555,49 @@
         def _():
             act_copy(k).start()
 
-        if k == 0:
-            rs_second()
-
-    for h in range(2):
-        arrived(pdr.at[0], 8 + h)
-        arrived(pdi.at[0], 6 + h)
-    for k in range(2):
+    def finish_saved():
         for a in range(2):
-            dinp[k, pl.ds(256 * a, 256), :] = (
-                pdr[k, a].astype(F32) + tn(f1[a], pdi[k, a])
-            ).astype(BF)
-
-        @pl.when(sec > 0)
-        def _():
-            grad_copy(k).start()
-
+            arrived(pdr.at[:, a], 8 + a)
+            arrived(pdi.at[:, a], 6 + a)
+            for k in range(2):
+                dinp[k, pl.ds(256 * a, 256), :] = (
+                    pdr[k, a].astype(F32) + tn(f1[a], pdi[k, a])
+                ).astype(BF)
+
+            @pl.when(sec > 0)
+            def _():
+                for k in range(2):
+                    grad_copy(k, a).start()
+
+    pl.semaphore_wait(barrier, 2 * NQ + 1)
+
+    send_v(0)
+    send_g(0)
+    lend()
+    factor_saved()
+    send_inner(0)
+    send_v(1)
+    send_g(1)
+    send_inner(1)
+    factor_fresh(0)
+    send_fresh(0)
+    factor_fresh(1)
+    send_fresh(1)
+    fact_fresh()
+    fact_saved()
+    saved(0)
+    second_fresh(0)
+    second_fresh(1)
+    saved(1)
+    gradients()
+    core_sums()
+    rs_first()
+    mix_fresh(0)
+    finish_saved()
+    rs_second()
+    mix_fresh(1)
     rs_third()
+
     for a in range(2):
         fg[a] = nt(pdi[0, a], vs[0, a]) + nt(pdi[1, a], vs[1, a])
     first_copy = remote(fg, fg_r, mxs.at[4], mxr.at[4], partner)
@@ -596,13 +636,17 @@
         stores.append(store(upo.at[slot], oup.at[slot], 4 + slot))
         stores.append(store(dno.at[slot], odn.at[slot], 6 + slot))
 
-    sent = ((pin_s, 0, 0), (vs, 2, 0), (gg, 4, 0), (cdi, 6, 1), (cdr, 8, 1), (pin_f, 10, 0), (cmx_f, 12, 1))
+    sent = ((pin_s, 0, 0), (vs, 2, 0), (gg, 4, 0), (cdi, 6, 2), (cdr, 8, 2), (pin_f, 10, 0), (cmx_f, 12, 1))
     for src, i, kind in sent:
         for k in range(2):
-            most = src.at[k, :, pl.ds(0, 240), :] if kind == 0 else src.at[k, pl.ds(0, 30)]
+            if kind == 0:
+                most, rest = src.at[k, :, pl.ds(0, 240), :], src.at[k, :, pl.ds(0, 16), :]
+            elif kind == 1:
+                most, rest = src.at[k, pl.ds(0, 30)], None
+            else:
+                most, rest = src.at[:, pl.ds(0, 15)], src.at[:, pl.ds(0, 1)]
             pltpu.make_async_copy(most, most, a2s.at[i + k]).wait()
             if i < 10:
-                rest = src.at[k, :, pl.ds(0, 16), :] if kind == 0 else src.at[k, pl.ds(0, 2)]
 
                 @pl.when(away)
                 def _():
@@ -631,13 +675,15 @@
     def _():
         for k in range(2):
             act_copy(k).wait_send()
-            grad_copy(k).wait_recv()
+            for a in range(2):
+                grad_copy(k, a).wait_recv()
 
     @pl.when(sec > 0)
     def _():
         for k in range(2):
-            grad_copy(k).wait_send()
             act_copy(k).wait_recv()
+            for a in range(2):
+                grad_copy(k, a).wait_send()
 
     @pl.when(sec == 0)
     def _():
@@ -733,7 +779,7 @@
             pltpu.VMEM((2, 16, HALF), F32),
             pltpu.VMEM((512, 32), F32),
             dma((14,)), dma((14,)), dma((14,)), dma((6,)), dma((5,)), dma((6,)), dma((6,)),
-            dma((5,)), dma((5,)), dma((4,)), dma((2, 2)), dma((4,)), dma((4,)),
+            dma((5,)), dma((5,)), dma((4,)), dma((2, 2)), dma((6,)), dma((6,)),
             dma((6,)), dma((6,)), dma((8,)),
         ],
         compiler_params=pltpu.CompilerParams(

time: 132 us -> 124 us (0.939)
  Pallas kernels: 131 us -> 123 us
    pallas_call x1, Pallas kernels: 128 us -> 120 us  [body(): pl.pallas_call(kernel, out_shape=shapes, in_specs=[any_space] * 8, out_sp...]
where the time goes in v3:
time: 124 us
  Pallas kernels  123 us (99%)
    pallas_call x1, Pallas kernels, body(): pl.pallas_call(kernel, out_shape=shapes, in_specs=[any_space] * 8, out_sp...  120 us
    pallas_call x1, Pallas kernels, body(): pl.pallas_call(hand_on, out_shape=shapes, in_specs=[any_space] * 7, out_s...  3.28 us

profile of v3, /device:TPU:1, one launch (start us, length us, event | category | flops | bytes accessed | tf_op | source)
XLA Modules:
  0.0 123.9 jit_solution(4412591835984587790)
XLA Ops:
  0.6 119.8 %shard_map.135 = (bf16[512,1024]{1,0:T(8,128)(2,1)}, bf16[512,1024]{1,0:T(8,128)(2,1)}, f32[2,32,2048]{2,1,0:T(8,128)}, f32[2,128,512]{2,1,0:T(8,128)}, f32[16,1...) custom-call(bf16[2,256,1024]{2,1,0:T(8,128)(2,1)} %bitcast.17, bf16[2,256,1024]{2,1,0:T(8,128)(2,1)} %bitcast.18, ...), custom_call_target="tpu_custom_call" | custom-call | tf_op jit(solution)/shard_map/pallas_call | solution.py:738
  120.5 3.3 %shard_map.136 = (bf16[512,1024]{1,0:T(8,128)(2,1)}, bf16[512,1024]{1,0:T(8,128)(2,1)}, f32[2,32,2048]{2,1,0:T(8,128)}, f32[2,128,512]{2,1,0:T(8,128)}, f32[16,1...) custom-call(bf16[512,1024]{1,0:T(8,128)(2,1)} %get-tuple-element.21.refs_0_, ...), custom_call_target="tpu_custom_call" | custom-call | tf_op jit(solution)/shard_map/pallas_call | solution.py:792

commit v4 on v3

--- a/solution.py
+++ b/solution.py
@@ -179,9 +179,6 @@
             dst[k, a] = nn(f1[a], v[k, a]).astype(BF)
 
     def send_v(h):
-        if h == 0:
-            for k in range(2):
-                l_vs[k].wait()
         scatter(column_piece, vs, cv, 2 + h, h)
 
     def send_g(h):
@@ -199,6 +196,7 @@
     def factor_saved():
         l_f1.wait()
         for k in range(2):
+            l_vs[k].wait()
             first_factor(vs, pin_s, k)
 
     def factor_fresh(k):
@@ -571,14 +569,14 @@
 
     pl.semaphore_wait(barrier, 2 * NQ + 1)
 
-    send_v(0)
-    send_g(0)
     lend()
     factor_saved()
     send_inner(0)
+    send_v(0)
+    send_g(0)
+    send_inner(1)
     send_v(1)
     send_g(1)
-    send_inner(1)
     factor_fresh(0)
     send_fresh(0)
     factor_fresh(1)
@@ -702,18 +700,21 @@
 def hand_on(*refs):
     count = (len(refs) - 1) // 3
     sems = refs[-1]
-    into = [
-        pltpu.make_async_copy(refs[i], refs[2 * count + i], sems.at[0, i]) for i in range(count)
-    ]
-    out = [
-        pltpu.make_async_copy(refs[2 * count + i], refs[count + i], sems.at[1, i])
-        for i in range(count)
-    ]
+    pieces = []
+    for i in range(count):
+        size = refs[i].shape[0]
+        cut = 128 if size == TOK else 1 if size == GRP else size
+        pieces += [(i, pl.ds(start, cut)) for start in range(0, size, cut)]
+    into, out = [], []
+    for n, (i, at) in enumerate(pieces):
+        held = refs[2 * count + i].at[at]
+        into.append(pltpu.make_async_copy(refs[i].at[at], held, sems.at[0, n]))
+        out.append(pltpu.make_async_copy(held, refs[count + i].at[at], sems.at[1, n]))
     for copy in into:
         copy.start()
-    for i in range(count):
-        into[i].wait()
-        out[i].start()
+    for first, second in zip(into, out):
+        first.wait()
+        second.start()
     for copy in out:
         copy.wait()
 
@@ -794,7 +795,7 @@
         out_shape=shapes,
         in_specs=[any_space] * 7,
         out_specs=(any_space,) * 7,
-        scratch_shapes=[pltpu.VMEM(part.shape, part.dtype) for part in shapes] + [dma((2, 7))],
+        scratch_shapes=[pltpu.VMEM(part.shape, part.dtype) for part in shapes] + [dma((2, 19))],
     )(*outs)
     return (
         act[None],

time: 124 us -> 124 us (level)
  no operation moved by 1% of the time
where the time goes in v4:
time: 124 us
  Pallas kernels  123 us (99%)
    pallas_call x1, Pallas kernels, body(): pl.pallas_call(kernel, out_shape=shapes, in_specs=[any_space] * 8, out_sp...  120 us
    pallas_call x1, Pallas kernels, body(): pl.pallas_call(hand_on, out_shape=shapes, in_specs=[any_space] * 7, out_s...  3.56 us

profile of v4, /device:TPU:1, one launch (start us, length us, event | category | flops | bytes accessed | tf_op | source)
XLA Modules:
  0.0 124.0 jit_solution(18213427776288108555)
XLA Ops:
  0.6 119.7 %shard_map.135 = (bf16[512,1024]{1,0:T(8,128)(2,1)}, bf16[512,1024]{1,0:T(8,128)(2,1)}, f32[2,32,2048]{2,1,0:T(8,128)}, f32[2,128,512]{2,1,0:T(8,128)}, f32[16,1...) custom-call(bf16[2,256,1024]{2,1,0:T(8,128)(2,1)} %bitcast.17, bf16[2,256,1024]{2,1,0:T(8,128)(2,1)} %bitcast.18, ...), custom_call_target="tpu_custom_call" | custom-call | tf_op jit(solution)/shard_map/pallas_call | solution.py:739
  120.3 3.6 %shard_map.136 = (bf16[512,1024]{1,0:T(8,128)(2,1)}, bf16[512,1024]{1,0:T(8,128)(2,1)}, f32[2,32,2048]{2,1,0:T(8,128)}, f32[2,128,512]{2,1,0:T(8,128)}, f32[16,1...) custom-call(bf16[512,1024]{1,0:T(8,128)(2,1)} %get-tuple-element.21.refs_0_, ...), custom_call_target="tpu_custom_call" | custom-call | tf_op jit(solution)/shard_map/pallas_call | solution.py:793
